TPU v7x, 256 devices: a whole 4x4x8 slice. The times are simulated.
256 devices in a mesh: phase: 2 (over core), batch: 8 (over z), seq: 16 (over y, x).
Axes of the slice: x: 4, y: 4, z: 8, core: 2. Of those that a mesh axis runs over, the one named last changes fastest.
Arguments:
- features: bfloat16 [8, 8192, 128], P('batch', 'seq'), may hold values from -6 to 6
- lengths: int32 [8, 12], P('batch'), may hold values from 1 to 256, 2048 in all within a row
- conv1_weight: float32 [3, 3, 256], replicated, may hold values from -2 to 2
- conv1_bias: float32 [256], replicated, may hold values from -3 to 3
- conv2_weight: bfloat16 [3, 3, 256, 256], P(None, None, None, 'phase'), may hold values from -0.125 to 0.125
- conv2_bias: float32 [256], P('phase'), may hold values from -3 to 3
- proj_weight: bfloat16 [8192, 1536], P(('phase', 'seq')), may hold values from -0.0625 to 0.0625
- proj_bias: float32 [1536], replicated, may hold values from -6 to 6
- norm_gain: float32 [1536], replicated, may hold values from 0.25 to 1.75
- qkv_weight: bfloat16 [1536, 3, 1536], P(None, None, 'phase'), may hold values from -1 to 1
- out_weight: bfloat16 [1536, 1536], P('phase'), may hold values from -0.15625 to 0.15625
Outputs:
- encoded: bfloat16 [8, 2048, 1536], P('batch', 'seq', 'phase')
Inputs may be any that keep to these rules, and one draw needn't show every extreme that they name: In each group the 12 lengths add up to 2048 and the largest is exactly 256; an utterance covers four times its length of input frames.
All inputs are finite; a program needn't handle non-finite values.
Results may differ from a plain program's by a relative error of at most 0.017.
Values may be sent and summed in bfloat16 or wider, within the bound.
A program may use at most 128 MiB of HBM per device.

v0:
```python
import math

import jax
import jax.numpy as jnp
from jax import lax
from jax.sharding import PartitionSpec as P

HEAD = 64
SPAN = 2


def shifted_2(value, axis, steps):
    count = lax.axis_size(axis)
    initial, last = (max(0, -steps), min(count, count - steps))
    return lax.ppermute(value, axis, [(source, source + steps) for source in range(initial, last)])


def segment_info(lengths_row, positions, group_len):
    offsets = jnp.cumsum(lengths_row, dtype=jnp.int32) - lengths_row
    starts = jnp.any(positions[:, None] == offsets[None, :], axis=1)
    inside = (positions >= 0) & (positions < group_len)
    counted = jnp.sum((positions[:, None] >= offsets[None, :]).astype(jnp.int32), axis=1) - 1
    return (starts, jnp.where(inside, counted, -1))


def first_conv(widened, kept, weights, biases):
    rows_in = widened.shape[0]
    rows_out = (rows_in - 3) // 2 + 1
    bins = widened.shape[1]
    half = bins // 2
    source = jnp.arange(bins, dtype=jnp.int32)[:, None]
    target = jnp.arange(3 * half, dtype=jnp.int32)[None, :]
    wanted = 2 * (target % half) + target // half - 1
    picker = (source == wanted).astype(jnp.float32)
    picked = jnp.dot(
        widened, picker, precision=lax.Precision.HIGHEST, preferred_element_type=jnp.float32
    )
    padded = jnp.concatenate([picked, jnp.zeros((1, 3 * half), jnp.float32)], axis=0)
    pairs = padded.reshape(rows_out + 1, 2, 3 * half)
    ones_row = jnp.ones_like(kept)
    row_mask = jnp.concatenate(
        [jnp.ones((1,), jnp.float32), jnp.stack([kept, ones_row], axis=1).reshape(-1)]
    )
    row_taps = [
        pairs[0:rows_out, 0] * row_mask[:, None],
        pairs[0:rows_out, 1],
        pairs[1 : rows_out + 1, 0],
    ]
    summed = jnp.zeros((rows_out, half, weights.shape[2]), jnp.float32) + biases
    for step_time in range(3):
        for step_bin in range(3):
            tapped = row_taps[step_time][:, step_bin * half : (step_bin + 1) * half]
            summed = summed + tapped[:, :, None] * weights[step_time, step_bin]
    return jax.nn.relu(summed).astype(jnp.bfloat16)


def second_conv(first_maps, kept, weights, biases):
    rows_in = first_maps.shape[0]
    frames_out = (rows_in - 1) // 2
    quarter = first_maps.shape[1] // 2
    channels = first_maps.shape[2]
    split = first_maps.reshape(rows_in, quarter, 2, channels)
    even_bins = split[:, :, 0]
    odd_bins = split[:, :, 1]
    shifted = jnp.concatenate(
        [jnp.zeros((rows_in, 1, channels), first_maps.dtype), odd_bins[:, :-1]], axis=1
    )
    bin_taps = [shifted, even_bins, odd_bins]
    kept_half = kept.astype(jnp.bfloat16)
    summed = jnp.zeros((frames_out * quarter, weights.shape[3]), jnp.float32)
    for step_bin in range(3):
        extended = jnp.concatenate(
            [bin_taps[step_bin], jnp.zeros((1, quarter, channels), first_maps.dtype)], axis=0
        )
        paired = extended.reshape(frames_out + 1, 2, quarter, channels)
        row_taps = [
            paired[0:frames_out, 0] * kept_half[:, None, None],
            paired[0:frames_out, 1],
            paired[1 : frames_out + 1, 0],
        ]
        for step_time in range(3):
            tapped = row_taps[step_time]
            summed = summed + jnp.dot(
                tapped.reshape(frames_out * quarter, channels),
                weights[step_time, step_bin],
                preferred_element_type=jnp.float32,
            )
    activated = jax.nn.relu(summed + biases).astype(jnp.bfloat16)
    return activated.reshape(frames_out, quarter, weights.shape[3])


def local(
    features,
    lengths,
    conv1_weight,
    conv1_bias,
    conv2_weight,
    conv2_bias,
    proj_weight,
    proj_bias,
    norm_gain,
    qkv_weight,
    out_weight,
):
    raw_rows = features[0]
    frames_dev = raw_rows.shape[0] // 4
    group_len = frames_dev * lax.axis_size("seq")
    seq_index = lax.axis_index("seq")
    lengths_row = lengths[0]
    positions = seq_index * frames_dev + jnp.arange(frames_dev, dtype=jnp.int32)
    starts, query_segment = segment_info(lengths_row, positions, group_len)
    kept = 1.0 - starts.astype(jnp.float32)
    left_rows = shifted_2(raw_rows[-3:], "seq", 1)
    widened = jnp.concatenate([left_rows, raw_rows], axis=0).astype(jnp.float32)
    first_maps = first_conv(widened, kept, conv1_weight, conv1_bias)
    second_maps = second_conv(first_maps, kept, conv2_weight, conv2_bias)
    flattened = second_maps.transpose(0, 2, 1).reshape(frames_dev, -1)
    partial_frames = jnp.dot(
        flattened,
        lax.all_gather(proj_weight, "seq", axis=0, tiled=True),
        preferred_element_type=jnp.float32,
    )
    summed = lax.psum(partial_frames, "phase")
    frames = (summed + proj_bias).astype(jnp.bfloat16)
    values32 = frames.astype(jnp.float32)
    average = jnp.mean(values32, axis=1, keepdims=True)
    centered = values32 - average
    variance = jnp.mean(centered * centered, axis=1, keepdims=True)
    normed = (centered * lax.rsqrt(variance + 1e-05) * norm_gain).astype(jnp.bfloat16)
    local_width = qkv_weight.shape[2]
    projected = jnp.dot(
        normed,
        qkv_weight.reshape(qkv_weight.shape[0], 3 * local_width),
        preferred_element_type=jnp.float32,
    ).astype(jnp.bfloat16)
    heads_here = local_width // HEAD
    query_heads = projected[:, :local_width].reshape(frames_dev, heads_here, HEAD)
    key_value = jnp.stack(
        [projected[:, local_width : 2 * local_width], projected[:, 2 * local_width :]]
    )
    scale = 1.0 / math.sqrt(HEAD)

    def attend(running, piece, start):
        rows_here = piece.shape[1]
        key_positions = start + jnp.arange(rows_here, dtype=jnp.int32)
        _, key_segment = segment_info(lengths_row, key_positions, group_len)
        same = query_segment[:, None] == key_segment[None, :]
        highest, denominator, numerator = running
        key_heads = piece[0].reshape(rows_here, heads_here, HEAD)
        value_heads = piece[1].reshape(rows_here, heads_here, HEAD)
        scores = (
            jnp.einsum("qhd,khd->hqk", query_heads, key_heads, preferred_element_type=jnp.float32)
            * scale
        )
        scores = jnp.where(same[None], scores, -1e30)
        new_highest = jnp.maximum(highest, jnp.max(scores, axis=2))
        factor = jnp.exp(highest - new_highest)
        weight = jnp.where(same[None], jnp.exp(scores - new_highest[:, :, None]), 0.0)
        denominator = denominator * factor + jnp.sum(weight, axis=2)
        numerator = numerator * factor[:, :, None] + jnp.einsum(
            "hqk,khd->hqd",
            weight.astype(jnp.bfloat16),
            value_heads,
            preferred_element_type=jnp.float32,
        )
        return (new_highest, denominator, numerator)

    initial = (
        jnp.full((heads_here, frames_dev), -1e30, jnp.float32),
        jnp.zeros((heads_here, frames_dev), jnp.float32),
        jnp.zeros((heads_here, frames_dev, HEAD), jnp.float32),
    )
    running = attend(initial, key_value, seq_index * frames_dev)
    for distance in list(range(1, SPAN + 1)) + list(range(-SPAN, 0)):
        arrived = shifted_2(key_value, "seq", distance)
        running = attend(running, arrived, (seq_index - distance) * frames_dev)
    _, denominator, numerator = running
    context = (
        (numerator / denominator[:, :, None])
        .transpose(1, 0, 2)
        .reshape(frames_dev, local_width)
        .astype(jnp.bfloat16)
    )
    branch = jnp.dot(context, out_weight, preferred_element_type=jnp.float32)
    half_width = branch.shape[1] // lax.axis_size("phase")
    reduced = lax.psum_scatter(
        branch.astype(jnp.bfloat16), "phase", scatter_dimension=1, tiled=True
    ).astype(jnp.float32)
    residual_part = lax.dynamic_slice_in_dim(
        values32, lax.axis_index("phase") * half_width, half_width, 1
    )
    return (residual_part + reduced).astype(jnp.bfloat16)[None]


def solution(mesh):
    in_specs = (
        P("batch", "seq", None),
        P("batch", None),
        P(),
        P(),
        P(None, None, None, "phase"),
        P("phase"),
        P(("phase", "seq"), None),
        P(),
        P(),
        P(None, None, "phase"),
        P("phase", None),
    )
    out_specs = P("batch", "seq", "phase")
    return jax.shard_map(local, mesh=mesh, in_specs=in_specs, out_specs=out_specs, check_vma=False)
```

profile of v0, /device:TPU:1, one launch (start us, length us, event | category | flops | bytes accessed | tf_op | source)
XLA Modules:
  0.0 239.7 jit_solution(5817431723094971448)
XLA Ops:
  8.0 3.9 %collective-permute-start = (bf16[3,128]{1,0:T(4,128)(2,1)S(1)}, bf16[3,128]{1,0:T(4,128)(2,1)S(1)}, u32[]{:S(2)}, u32[]{:S(2)}) collective-permute-start(bf16[3,128]{1,0:T(4,128)(2,1)S(1)} %slice_bitcast_fusion.2), channel_id=1, source_target_pairs={{0,1},{1,2},{2,3},{3,4},{4,5},{5,6},{6,7},{7,8},{8,9},{9,10},{10,1... | collective-permute-start | bytes 2312 | tf_op jit(solution)/shard_map/ppermute | solution.py:15
  28.6 1.8 copy.119
  32.1 1.8 copy.121
  43.4 1.8 copy.127
  45.1 22.0 %maximum_convert_fusion = bf16[257,32,2,256]{3,1,0,2:T(8,128)(2,1)S(1)} fusion(f32[256]{0:T(256)} %bitcast.304, f32[257,32,2]{1,0,2:T(8,128)} %copy.127, f32[256]{0:T(256)} %bitcast.305, f32[257,32,2]{1,0,2:T(8,128)} %copy.125, f32[256]{0:T(256)S(1)} %bitcast.298, f32[257,32,2]{1,0,2:T(8,128)} %copy.123, f32[256]{0:T(256)S(1)} %bitcast.299, ...), kind=kLoop, calls=%fused_computation | loop fusion | flops 84213760 | bytes 9023744 | tf_op jit(solution)/shard_map/convert_element_type | solution.py:54
  68.6 2.5 %pad.12 = bf16[258,32,256]{2,1,0:T(8,128)(2,1)S(1)} pad(bf16[257,31,256]{2,1,0:T(8,128)(2,1)S(1)} %bitcast.264, bf16[]{:T(256)} %constant.98.clone.1), padding=0_1x1_0x0_0 | pad | bytes 8306178 | tf_op jit(solution)/shard_map/concatenate | solution.py:72
  80.3 1.8 fusion.2
  82.1 2.5 %copy.128 = bf16[128,32,128]{0,1,2:T(8,128)(2,1)S(1)} copy(bf16[128,32,128]{2,1,0:T(8,128)(2,1)} %bitcast.284) | data formatting | bytes 2097152 | tf_op jit(solution)/shard_map/reshape | solution.py:89
  84.6 24.1 %all-gather.2.cloned.1.call-done = bf16[4096,1536]{1,0:T(8,128)(2,1)} async-done(((bf16[256,1536]{1,0:T(8,128)(2,1)}), bf16[4096,1536]{1,0:T(8,128)(2,1)}) %all-gather.2.cloned.1.call-update) | async-done | bytes 12582928 | tf_op jit(solution)/shard_map/all_gather | solution.py:120
  108.6 7.4 %fusion.121 = f32[128,1536]{1,0:T(8,128)} fusion(bf16[128,4096]{0,1:T(8,128)(2,1)S(1)} %bitcast.283, bf16[4096,1536]{1,0:T(8,128)(2,1)} %all-gather.2.cloned.1.call-done), kind=kOutput, calls=%fused_computation.203 | convolution fusion | flops 1610612736 | bytes 14417920 | tf_op jit(solution)/shard_map/dot_general | solution.py:118
  116.2 10.3 %copy.129 = bf16[1536,3,768]{0,2,1:T(8,128)(2,1)} copy(bf16[1536,3,768]{2,0,1:T(8,128)(2,1)} %param.20) | data formatting | bytes 14155776 | tf_op args[9]
  126.6 20.0 %all-reduce.8.cloned.1.call-done = f32[128,1536]{1,0:T(8,128)} async-done(((f32[128,1536]{1,0:T(8,128)}), f32[128,1536]{1,0:T(8,128)}) %all-reduce.8.cloned.1.call-update) | async-done | bytes 786448 | tf_op jit(solution)/shard_map/psum | solution.py:123
  146.7 2.1 fusion.99
  149.2 5.4 %convolution_convert_fusion = bf16[128,2304]{1,0:T(8,128)(2,1)S(1)} fusion(bf16[1536,2304]{0,1:T(8,128)(2,1)} %bitcast.265, bf16[128,1536]{1,0:T(8,128)(2,1)S(1)} %get-tuple-element.11, f32[1536]{0:T(1024)S(1)} %copy-done.33, f32[128]{0:T(128)S(1)} %add_rsqrt_fusion, f32[128]{0:T(128)S(1)} %broadcast_multiply_fusion), kind=kOutput, calls=%fused_computation.14 | convolution fusion | flops 907247616 | bytes 8068096 | tf_op jit(solution)/shard_map/dot_general | solution.py:131
  155.5 3.6 %collective-permute-start.1 = (bf16[2,128,768]{2,1,0:T(8,128)(2,1)}, bf16[2,128,768]{2,1,0:T(8,128)(2,1)}, u32[]{:S(2)}, u32[]{:S(2)}) collective-permute-start(bf16[2,128,768]{2,1,0:T(8,128)(2,1)} %pad_maximum_fusion), channel_id=1, source_target_pairs={{0,1},{1,2},{2,3},{3,4},{4,5},{5,6},{6,7},{7,8},{8,9},{9,10},{10,1... | collective-permute-start | bytes 1179656 | tf_op jit(solution)/shard_map/ppermute | solution.py:15
  159.9 4.3 %collective-permute-start.2 = (bf16[2,128,768]{2,1,0:T(8,128)(2,1)}, bf16[2,128,768]{2,1,0:T(8,128)(2,1)}, u32[]{:S(2)}, u32[]{:S(2)}) collective-permute-start(bf16[2,128,768]{2,1,0:T(8,128)(2,1)} %pad_maximum_fusion), channel_id=1, source_target_pairs={{0,2},{1,3},{2,4},{3,5},{4,6},{5,7},{6,8},{7,9},{8,10},{9,11},{10,... | collective-permute-start | bytes 1179656 | tf_op jit(solution)/shard_map/ppermute | solution.py:15
  168.2 1.8 fusion.120
  171.9 3.5 %collective-permute-done.2 = bf16[2,128,768]{2,1,0:T(8,128)(2,1)} collective-permute-done((bf16[2,128,768]{2,1,0:T(8,128)(2,1)}, bf16[2,128,768]{2,1,0:T(8,128)(2,1)}, u32[]{:S(2)}, u32[]{:S(2)}) %collective-permute-start.2) | collective-permute-done | bytes 393248 | tf_op jit(solution)/shard_map/ppermute | solution.py:15
  177.3 9.7 %collective-permute-done.3 = bf16[2,128,768]{2,1,0:T(8,128)(2,1)} collective-permute-done((bf16[2,128,768]{2,1,0:T(8,128)(2,1)}, bf16[2,128,768]{2,1,0:T(8,128)(2,1)}, u32[]{:S(2)}, u32[]{:S(2)}) %collective-permute-start.3) | collective-permute-done | bytes 393248 | tf_op jit(solution)/shard_map/ppermute | solution.py:15
  194.6 2.0 fusion.117
  196.5 1.9 fusion.116
  203.5 1.9 fusion.27
  205.4 2.2 convolution_bitcast_fusion
  215.5 16.1 %reduce-scatter.2.cloned.1.call-done = bf16[128,768]{1,0:T(8,128)(2,1)} async-done(((bf16[128,1536]{1,0:T(8,128)(2,1)}), bf16[128,768]{1,0:T(8,128)(2,1)}) %reduce-scatter.2.cloned.1.call-update) | async-done | bytes 196624 | tf_op jit(solution)/shard_map/reduce_scatter | solution.py:186
  (198 shorter events, 71.7 us)
Async XLA Ops:
  6.5 207.7 %copy-start = (bf16[768,1536]{1,0:T(8,128)(2,1)S(1)}, bf16[768,1536]{1,0:T(8,128)(2,1)}, u32[]{:S(2)}) copy-start(bf16[768,1536]{1,0:T(8,128)(2,1)} %param.21) | copy-start | bytes 7077892
  6.5 102.1 %all-gather.2.cloned.1.call-start = ((), (), s32[]{:S(2)}) async-start(), calls=%async_computation.1 | async-start | bytes 13369344 | tf_op jit(solution)/shard_map/all_gather | solution.py:120
  7.3 139.4 %all-reduce.8.cloned.1.call-start = ((), (), s32[]{:S(2)}) async-start(), calls=%async_computation.2 | async-start | bytes 1572864 | tf_op jit(solution)/shard_map/psum | solution.py:123
  8.0 9.5 %collective-permute-start = (bf16[3,128]{1,0:T(4,128)(2,1)S(1)}, bf16[3,128]{1,0:T(4,128)(2,1)S(1)}, u32[]{:S(2)}, u32[]{:S(2)}) collective-permute-start(bf16[3,128]{1,0:T(4,128)(2,1)S(1)} %slice_bitcast_fusion.2), channel_id=1, source_target_pairs={{0,1},{1,2},{2,3},{3,4},{4,5},{5,6},{6,7},{7,8},{8,9},{9,10},{10,1... | collective-permute-start | bytes 2312 | tf_op jit(solution)/shard_map/ppermute | solution.py:15
  34.6 10.5 %copy-start.4 = (f32[257,32,2]{1,0,2:T(8,128)S(1)}, f32[257,32,2]{1,0,2:T(8,128)}, u32[]{:S(2)}) copy-start(f32[257,32,2]{1,0,2:T(8,128)} %copy.117) | copy-start | bytes 197380
  116.0 115.5 %reduce-scatter.2.cloned.1.call-start = ((), (), s32[]{:S(2)}) async-start(), calls=%async_computation.3 | async-start | bytes 589824 | tf_op jit(solution)/shard_map/reduce_scatter | solution.py:186
  116.1 10.4 %copy-start.36 = (s32[128]{0:T(128)S(1)}, s32[128]{0:T(128)}, u32[]{:S(2)}) copy-start(s32[128]{0:T(128)} %copy-done.35) | copy-start | bytes 1540
  116.1 10.4 %copy-start.38 = (s32[12]{0:T(128)S(1)}, s32[12]{0:T(128)}, u32[]{:S(2)}) copy-start(s32[12]{0:T(128)} %copy-done.37) | copy-start | bytes 148
  116.1 10.4 %copy-start.39 = (s32[128]{0:T(128)S(1)}, s32[128]{0:T(128)}, u32[]{:S(2)}) copy-start(s32[128]{0:T(128)} %iota_add_fusion) | copy-start | bytes 1540
  116.1 10.3 %copy-start.40 = (s32[128]{0:T(128)S(1)}, s32[128]{0:T(128)}, u32[]{:S(2)}) copy-start(s32[128]{0:T(128)} %iota_add_fusion.1) | copy-start | bytes 1540
  116.1 10.3 %copy-start.41 = (s32[128]{0:T(128)S(1)}, s32[128]{0:T(128)}, u32[]{:S(2)}) copy-start(s32[128]{0:T(128)} %iota_add_fusion.2) | copy-start | bytes 1540
  116.1 30.5 %copy-start.32 = (f32[1536]{0:T(1024)S(1)}, f32[1536]{0:T(1024)}, u32[]{:S(2)}) copy-start(f32[1536]{0:T(1024)} %param.18) | copy-start | bytes 18436
  126.5 22.7 %copy-start.33 = (f32[1536]{0:T(1024)S(1)}, f32[1536]{0:T(1024)}, u32[]{:S(2)}) copy-start(f32[1536]{0:T(1024)} %param.19) | copy-start | bytes 18436
  155.5 14.4 %collective-permute-start.1 = (bf16[2,128,768]{2,1,0:T(8,128)(2,1)}, bf16[2,128,768]{2,1,0:T(8,128)(2,1)}, u32[]{:S(2)}, u32[]{:S(2)}) collective-permute-start(bf16[2,128,768]{2,1,0:T(8,128)(2,1)} %pad_maximum_fusion), channel_id=1, source_target_pairs={{0,1},{1,2},{2,3},{3,4},{4,5},{5,6},{6,7},{7,8},{8,9},{9,10},{10,1... | collective-permute-start | bytes 1179656 | tf_op jit(solution)/shard_map/ppermute | solution.py:15
  159.9 16.6 %copy-start.12 = (pred[128,128]{0,1:T(8,128)(4,1)}, pred[128,128]{0,1:T(8,128)(4,1)S(1)}, u32[]{:S(2)}) copy-start(pred[128,128]{0,1:T(8,128)(4,1)S(1)} %get-tuple-element.68) | copy-start | bytes 49156
  159.9 15.5 %collective-permute-start.2 = (bf16[2,128,768]{2,1,0:T(8,128)(2,1)}, bf16[2,128,768]{2,1,0:T(8,128)(2,1)}, u32[]{:S(2)}, u32[]{:S(2)}) collective-permute-start(bf16[2,128,768]{2,1,0:T(8,128)(2,1)} %pad_maximum_fusion), channel_id=1, source_target_pairs={{0,2},{1,3},{2,4},{3,5},{4,6},{5,7},{6,8},{7,9},{8,10},{9,11},{10,... | collective-permute-start | bytes 1179656 | tf_op jit(solution)/shard_map/ppermute | solution.py:15
  164.2 22.8 %collective-permute-start.3 = (bf16[2,128,768]{2,1,0:T(8,128)(2,1)}, bf16[2,128,768]{2,1,0:T(8,128)(2,1)}, u32[]{:S(2)}, u32[]{:S(2)}) collective-permute-start(bf16[2,128,768]{2,1,0:T(8,128)(2,1)} %pad_maximum_fusion), channel_id=1, source_target_pairs={{2,0},{3,1},{4,2},{5,3},{6,4},{7,5},{8,6},{9,7},{10,8},{11,9},{12,... | collective-permute-start | bytes 1179656 | tf_op jit(solution)/shard_map/ppermute | solution.py:15
  165.5 24.0 %collective-permute-start.4 = (bf16[2,128,768]{2,1,0:T(8,128)(2,1)}, bf16[2,128,768]{2,1,0:T(8,128)(2,1)}, u32[]{:S(2)}, u32[]{:S(2)}) collective-permute-start(bf16[2,128,768]{2,1,0:T(8,128)(2,1)} %pad_maximum_fusion), channel_id=1, source_target_pairs={{1,0},{2,1},{3,2},{4,3},{5,4},{6,5},{7,6},{8,7},{9,8},{10,9},{11,1... | collective-permute-start | bytes 1179656 | tf_op jit(solution)/shard_map/ppermute | solution.py:15
  193.2 6.6 %copy-start.21 = (f32[12,128]{1,0:T(8,128)}, f32[12,128]{1,0:T(8,128)S(1)}, u32[]{:S(2)}) copy-start(f32[12,128]{1,0:T(8,128)S(1)} %get-tuple-element.81) | copy-start | bytes 18436
  193.2 5.2 %copy-start.19 = (f32[12,128]{1,0:T(8,128)S(1)}, f32[12,128]{1,0:T(8,128)}, u32[]{:S(2)}) copy-start(f32[12,128]{1,0:T(8,128)} %get-tuple-element.83) | copy-start | bytes 18436
  193.2 5.8 %copy-start.14 = (pred[128,128]{0,1:T(8,128)(4,1)S(1)}, pred[128,128]{0,1:T(8,128)(4,1)}, u32[]{:S(2)}) copy-start(pred[128,128]{0,1:T(8,128)(4,1)} %get-tuple-element.69) | copy-start | bytes 49156
  193.2 6.6 %copy-start.9 = (bf16[1,128,768]{1,2,0:T(8,128)(2,1)S(1)}, bf16[1,128,768]{1,2,0:T(8,128)(2,1)}, u32[]{:S(2)}) copy-start(bf16[1,128,768]{1,2,0:T(8,128)(2,1)} %copy.138) | copy-start | bytes 589828
  194.5 5.3 %copy-start.23 = (f32[12,128]{1,0:T(8,128)}, f32[12,128]{1,0:T(8,128)S(1)}, u32[]{:S(2)}) copy-start(f32[12,128]{1,0:T(8,128)S(1)} %get-tuple-element.79) | copy-start | bytes 18436
  214.2 17.4 %copy-start.3 = (f32[128,1536]{1,0:T(8,128)S(1)}, f32[128,1536]{1,0:T(8,128)}, u32[]{:S(2)}) copy-start(f32[128,1536]{1,0:T(8,128)} %get-tuple-element.10) | copy-start | bytes 2359300
  (26 other events, 74.4 us)
Sparse Core Ops, SparseCore 0:
  9.8 98.8 all-gather.1
  116.2 30.4 all-reduce.7
  215.6 15.9 reduce-scatter.1
where the time goes:
time: 241 us; the launch traced here: 240 us
  waiting for transfers between devices  74.1 us (31%)
  local copies, waits for them, and re-layouts  62.9 us (26%)
  other arithmetic  40.9 us (17%)
  matrix products  33.2 us (14%)
  starting transfers between devices  14.7 us (6%)
  between operations  13.9 us (6%)
    all_gather x1, waiting for transfers between devices, local(): lax.all_gather(proj_weight, 'seq', axis=0, tiled=True)  24.1 us
    convert_element_type x1, other arithmetic, first_conv(): return jax.nn.relu(summed).astype(jnp.bfloat16)  22 us
    psum x1, waiting for transfers between devices, local(): summed = lax.psum(partial_frames, 'phase')  20 us
    reduce_scatter x1, waiting for transfers between devices, local(): lax.psum_scatter(branch.astype(jnp.bfloat16), 'phase', scatter_dimension=...  16.1 us
    mul x18, local copies, waits for them, and re-layouts, first_conv(): summed = summed + tapped[:, :, None] * weights[step_time, step_bin]  15.4 us
    ppermute x5, starting transfers between devices, shifted_2(): lax.ppermute(value, axis, [(source, source + steps) for source in range(i...  14.7 us
    ppermute x5, waiting for transfers between devices, shifted_2(): lax.ppermute(value, axis, [(source, source + steps) for source in range(i...  13.2 us
    unnamed x87, local copies, waits for them, and re-layouts  12.4 us
  transfers between devices with their start and end apart: 8, of which 5 were waited for; matrix products, arithmetic and copies ran while one was open for 39% of the time, Pallas kernels for 0%

commit v1 on v0

v1 whole, which is shorter than its diff:
```python
import math

import jax
import jax.numpy as jnp
import numpy as np
from jax import lax
from jax.experimental import pallas as pl
from jax.experimental.pallas import tpu as pltpu
from jax.sharding import PartitionSpec as P

MESH = pl.DeviceIdType.MESH
BF16 = jnp.bfloat16
F32 = jnp.float32

SIDE = 4
BLOCKS = SIDE * SIDE
FRAMES = 128
HALF = 64
BINS = 32
UTTS = 12
WIDTH = 1536
LOCAL = 768
HEAD = 64
EVEN = 144
ROWS = EVEN + FRAMES
PADDED = 584
TILES = 8
CUT = 256
CUTS = WIDTH // CUT
REACH = 2
SPAN = (2 * REACH + 1) * FRAMES
NEAR = (-2, -1, 1, 2)


def dot(a, b):
    return jnp.dot(a, b, preferred_element_type=F32)


def body(
    lengths_ref,
    feat_ref,
    w1_ref,
    b1_ref,
    w2_ref,
    b2_ref,
    wp_ref,
    pb_ref,
    gain_ref,
    qkv_ref,
    wo_ref,
    out_ref,
    halo,
    padded,
    picker,
    base,
    taps,
    patches,
    w2_even,
    w2_odd,
    fe,
    fo,
    w_all,
    maps_out,
    maps_in,
    part,
    sib_out,
    sib_in,
    tot,
    rs_out,
    rs_in,
    frames_mine,
    frames_cols,
    normed,
    qkv_w,
    out_w,
    query,
    keys,
    values,
    bias_mask,
    context,
    br_out,
    br_in,
    w2_sem,
    qkv_sem,
    out_sem,
    halo_send,
    halo_recv,
    w_send,
    w_recv,
    m_send,
    m_recv,
    sib_send,
    sib_recv,
    rs_send,
    rs_recv,
    fr_send,
    fr_recv,
    n_send,
    n_recv,
    own_send,
    own_recv,
    fw_send,
    fw_recv,
    br_send,
    br_recv,
):
    phase = lax.axis_index("phase")
    block = lax.axis_index("seq")
    x = block % SIDE
    y = block // SIDE
    other = 1 - phase

    def row_peer(dx):
        return y * SIDE + (x + dx) % SIDE

    def column_peer(dy):
        return ((y + dy) % SIDE) * SIDE + x

    def near_peer(d):
        return (block + d + BLOCKS) % BLOCKS

    def remote(src, dst, send, recv, target):
        return pltpu.make_async_remote_copy(
            src_ref=src,
            dst_ref=dst,
            send_sem=send,
            recv_sem=recv,
            device_id=target,
            device_id_type=MESH,
        )

    local_w2 = []
    for b in range(3):
        rows = pl.ds(b * 256, 256)
        local_w2.append(
            pltpu.make_async_copy(w2_ref.at[0, b], w2_even.at[rows, pl.ds(0, 128)], w2_sem.at[b])
        )
        local_w2.append(
            pltpu.make_async_copy(
                w2_ref.at[2, b], w2_even.at[rows, pl.ds(128, 128)], w2_sem.at[3 + b]
            )
        )
        local_w2.append(pltpu.make_async_copy(w2_ref.at[1, b], w2_odd.at[rows], w2_sem.at[6 + b]))
    for copy in local_w2:
        copy.start()
    qkv_copy = pltpu.make_async_copy(qkv_ref, qkv_w, qkv_sem)
    out_copy = pltpu.make_async_copy(wo_ref, out_w, out_sem)
    qkv_copy.start()
    out_copy.start()

    barrier = pltpu.get_barrier_semaphore()
    peers = [{"phase": other}]
    peers += [{"seq": row_peer(dx)} for dx in range(1, SIDE)]
    peers += [{"seq": column_peer(dy)} for dy in range(1, SIDE)]
    peers += [{"seq": near_peer(d)} for d in NEAR]
    for peer in peers:
        pl.semaphore_signal(barrier, inc=1, device_id=peer, device_id_type=MESH)

    out_row = lax.broadcasted_iota(jnp.int32, (256, 256), 0)
    in_row = lax.broadcasted_iota(jnp.int32, (256, 256), 1)
    reorder = jnp.where(in_row == (out_row & 7) * BINS + (out_row >> 3), 1.0, 0.0).astype(BF16)
    own_rows = pl.ds(pl.multiple_of(y * 32, 32), 32)
    for n in range(CUTS):
        cols = slice(n * CUT, (n + 1) * CUT)
        moved = dot(reorder, wp_ref[:, cols]).astype(BF16)
        for g in range(TILES):
            w_all[g, own_rows, cols] = moved[g * 32 : (g + 1) * 32]

    pl.semaphore_wait(barrier, len(peers))

    halo_copy = remote(
        feat_ref.at[pl.ds(496, 16)], halo, halo_send, halo_recv, {"seq": near_peer(1)}
    )
    halo_copy.start()
    w_copies = []
    for dy in range(1, SIDE):
        w_copies.append(
            remote(
                w_all.at[:, own_rows, :],
                w_all.at[:, own_rows, :],
                w_send.at[dy - 1],
                w_recv.at[dy - 1],
                {"seq": column_peer(dy)},
            )
        )
    for k in (0, 2, 1):
        w_copies[k].start()

    offsets = []
    running = jnp.int32(0)
    for i in range(UTTS):
        offsets.append(running)
        running = running + lengths_ref[0, i]
    place = lax.broadcasted_iota(jnp.int32, (FRAMES, 128), 0) + block * FRAMES
    starts = place == offsets[0]
    seg_query = jnp.where(place >= offsets[0], 1, 0)
    for off in offsets[1:]:
        starts = starts | (place == off)
        seg_query = seg_query + jnp.where(place >= off, 1, 0)
    kept = jnp.where(starts, 0.0, 1.0)
    key_place = lax.broadcasted_iota(jnp.int32, (8, SPAN), 1) + (block - REACH) * FRAMES
    seg_key = jnp.where(key_place >= offsets[0], 1, 0)
    for off in offsets[1:]:
        seg_key = seg_key + jnp.where(key_place >= off, 1, 0)
    seg_key = jnp.where((key_place >= 0) & (key_place < BLOCKS * FRAMES), seg_key, 0)
    for j in range(SPAN // 128):
        cols = slice(j * 128, (j + 1) * 128)
        bias_mask[:, cols] = jnp.where(seg_query == seg_key[0:1, cols], 0.0, -1e30)

    base[...] = jnp.zeros_like(base)
    for a in range(3):
        for b in range(3):
            for shift in range(3):
                row = 8 * a + 2 * shift + b
                base[row : row + 1, shift * 256 : (shift + 1) * 256] = w1_ref[a, b : b + 1, :]
    bias1 = b1_ref[...]
    high = bias1.astype(BF16).astype(F32)
    middle = (bias1 - high).astype(BF16).astype(F32)
    for k, piece in enumerate((high, middle, bias1 - high - middle)):
        base[24 + k : 25 + k, 0:256] = piece
        base[8 * k + 7 : 8 * k + 8, 256:512] = piece
        base[8 * k + 7 : 8 * k + 8, 512:768] = piece
    taps[...] = jnp.zeros_like(taps)
    for r in range(4):
        taps[r, 32 * r : 32 * r + 32, :] = base[...].astype(BF16)

    bins_in = lax.broadcasted_iota(jnp.int32, (128, BINS * 32), 0)
    lane = lax.broadcasted_iota(jnp.int32, (128, BINS * 32), 1)
    tap_bin = lane & 7
    tap_time = (lane >> 3) & 3
    hit = (bins_in == ((lane >> 5) * 4 + tap_bin - 3)) & (tap_bin < 7)
    for a in range(3):
        picker[a * 128 : (a + 1) * 128, :] = jnp.where(hit & (tap_time == a), 1.0, 0.0).astype(BF16)
    lane1 = lax.broadcasted_iota(jnp.int32, (1, BINS * 32), 1)
    low = lane1 & 31
    constant = ((low & 7) == 7) & (low < 24)
    constant = constant | ((low >= 24) & (low < 27) & (lane1 >= 32))
    constant = jnp.where(constant, 1.0, 0.0)

    padded[8:520, :] = feat_ref[...].astype(F32)
    padded[520:PADDED, :] = jnp.zeros((PADDED - 520, 128), F32)
    halo_copy.wait_recv()
    first = jnp.where(block > 0, 1.0, 0.0)
    padded[0:8, :] = halo[...].astype(F32)[8:16] * first
    even = [padded[pl.ds(5 + a, EVEN, stride=4), :] for a in range(3)]
    odd = [padded[pl.ds(7 + a, FRAMES, stride=4), :] for a in range(3)]
    odd[0] = odd[0] * kept
    gathered = jnp.concatenate(
        [jnp.concatenate(even, axis=1), jnp.concatenate(odd, axis=1)], axis=0
    ).astype(BF16)
    for k in range(4):
        cols = slice(k * 256, (k + 1) * 256)
        made = (dot(gathered, picker[:, cols]) + constant[:, cols]).astype(BF16)
        patches[2 * k] = made[:, 0:128]
        patches[2 * k + 1] = made[:, 128:256]

    for copy in local_w2:
        copy.wait()

    lane_slot = (lax.broadcasted_iota(jnp.int32, (FRAMES, 128), 1) >> 3) & 3
    bias2 = b2_ref[...]

    def maps_copy(dx, g):
        return remote(
            maps_out.at[(x + dx) % SIDE, g],
            maps_in.at[x, g],
            m_send.at[dx - 1, g],
            m_recv.at[dx - 1, g],
            {"seq": row_peer(dx)},
        )

    def convolve(g, carry):
        patch = patches[g]
        for r in range(4):
            for shift in range(3):
                cols = slice(shift * 256, (shift + 1) * 256)
                first_map = jnp.maximum(dot(patch, taps[r, :, cols]), 0.0).astype(BF16)
                fe[r * EVEN : (r + 1) * EVEN, cols] = first_map[:EVEN]
                fo[r * FRAMES : (r + 1) * FRAMES, cols] = first_map[EVEN:]
        second = []
        for r in range(4):
            sums = dot(fe[r * EVEN : (r + 1) * EVEN, :], w2_even[...])
            sums_odd = dot(fo[r * FRAMES : (r + 1) * FRAMES, :], w2_odd[...])
            later = pltpu.roll(sums[:, 128:256], EVEN - 1, 0)[:FRAMES]
            total = sums[:FRAMES, 0:128] * kept + later + sums_odd + bias2
            second.append(jnp.maximum(total, 0.0))
        for to in range(SIDE):
            mixed = second[to]
            for r in range(4):
                if r != to:
                    turned = pltpu.roll(second[r], (8 * (r - to)) % 128, 1)
                    mixed = jnp.where(lane_slot == r, turned, mixed)
            maps_out[to, g] = mixed.astype(BF16)
        for dx in (2, 1, 3):
            maps_copy(dx, g).start()
        return carry

    lax.fori_loop(0, TILES, convolve, 0)

    for g in range(TILES):
        maps_in[x, g] = maps_out[x, g]

    def maps_wait(g, carry):
        for dx in range(1, SIDE):
            maps_copy(dx, g).wait_recv()
        return carry

    lax.fori_loop(0, TILES, maps_wait, 0)
    for copy in w_copies:
        copy.wait_recv()

    mine = pl.ds(pl.multiple_of(phase * HALF, HALF), HALF)
    theirs = pl.ds(pl.multiple_of(other * HALF, HALF), HALF)

    def sib_copy(n):
        return remote(
            sib_out.at[n], sib_in.at[n], sib_send.at[n], sib_recv.at[n], {"phase": other}
        )

    def rs_copy(dx, n):
        return remote(
            rs_out.at[n, (x + dx) % SIDE],
            rs_in.at[dx - 1, n],
            rs_send.at[dx - 1, n],
            rs_recv.at[dx - 1, n],
            {"seq": row_peer(dx)},
        )

    def project(n):
        cols = pl.ds(pl.multiple_of(n * CUT, CUT), CUT)
        maps = jnp.concatenate(
            [
                jnp.concatenate([maps_in[s, g] for g in range(TILES)], axis=1)
                for s in range(SIDE)
            ],
            axis=0,
        )
        weights = w_all[:, :, cols].reshape(TILES * 128, CUT)
        part[n] = dot(maps, weights).reshape(SIDE, FRAMES, CUT)
        sib_out[n] = part[n, :, theirs, :].astype(BF16)
        sib_copy(n).start()

    def pass_on(n):
        sib_copy(n).wait_recv()
        both = part[n, :, mine, :] + sib_in[n].astype(F32)
        tot[n] = both
        rs_out[n] = both.astype(BF16)
        for dx in (2, 1, 3):
            rs_copy(dx, n).start()

    def project_step(n, carry):
        @pl.when(n < CUTS)
        def _():
            project(n)

        @pl.when(n >= 2)
        def _():
            pass_on(n - 2)

        return carry

    lax.fori_loop(0, CUTS + 2, project_step, 0)

    for n in range(CUTS):
        cols = slice(n * CUT, (n + 1) * CUT)
        for dx in range(1, SIDE):
            rs_copy(dx, n).wait_recv()
        total = tot[n, x]
        for dx in range(1, SIDE):
            total = total + rs_in[dx - 1, n].astype(F32)
        frames_mine[:, cols] = (total + pb_ref[:, cols]).astype(BF16)
    frames_copy = remote(
        frames_mine.at[:, pl.ds(pl.multiple_of(other * LOCAL, LOCAL), LOCAL)],
        frames_cols.at[mine, :],
        fr_send,
        fr_recv,
        {"phase": other},
    )
    frames_copy.start()
    numbers = frames_mine[...].astype(F32)
    average = jnp.mean(numbers, axis=1, keepdims=True)
    centered = numbers - average
    variance = jnp.mean(centered * centered, axis=1, keepdims=True)
    own_slot = pl.ds(pl.multiple_of(REACH * FRAMES + phase * HALF, HALF), HALF)
    normed[own_slot, :] = (centered * lax.rsqrt(variance + 1e-05) * gain_ref[...]).astype(BF16)

    def slot(d):
        return pl.ds(pl.multiple_of((REACH + d) * FRAMES + phase * HALF, HALF), HALF)

    near = []
    forward = []
    for k, d in enumerate(NEAR):
        near.append(
            remote(
                normed.at[own_slot, :],
                normed.at[slot(d), :],
                n_send.at[k],
                n_recv.at[k],
                {"seq": near_peer(-d)},
            )
        )
        forward.append(
            remote(
                normed.at[slot(d), :],
                normed.at[slot(d), :],
                fw_send.at[k],
                fw_recv.at[k],
                {"phase": other},
            )
        )
    own_copy = remote(
        normed.at[own_slot, :], normed.at[own_slot, :], own_send, own_recv, {"phase": other}
    )
    for k in (0, 3, 1, 2):
        near[k].start()
    own_copy.start()
    frames_cols[mine, :] = frames_mine[:, pl.ds(pl.multiple_of(phase * LOCAL, LOCAL), LOCAL)]
    qkv_copy.wait()
    out_copy.wait()
    own_copy.wait_recv()

    def keys_values(low, rows):
        block_rows = normed[low : low + rows, :]
        for n in range(3):
            cols = slice(n * CUT, (n + 1) * CUT)
            keys[low : low + rows, cols] = dot(block_rows, qkv_w[1, :, cols]).astype(BF16)
            values[low : low + rows, cols] = dot(block_rows, qkv_w[2, :, cols]).astype(BF16)

    own_low = REACH * FRAMES
    own_block = normed[own_low : own_low + FRAMES, :]
    for n in range(3):
        cols = slice(n * CUT, (n + 1) * CUT)
        made = dot(own_block, qkv_w[0, :, cols]).astype(BF16)
        query[:, cols] = made * jnp.asarray(1.0 / math.sqrt(HEAD), BF16)
    keys_values(own_low, FRAMES)
    for k in (1, 2):
        near[k].wait_recv()
        forward[k].start()
    for k in (1, 2):
        forward[k].wait_recv()
    keys_values(FRAMES, FRAMES)
    keys_values(3 * FRAMES, FRAMES)
    for k in (0, 3):
        near[k].wait_recv()
        forward[k].start()
    for k in (0, 3):
        forward[k].wait_recv()
    keys_values(0, FRAMES)
    keys_values(4 * FRAMES, FRAMES)

    lane_low = lax.broadcasted_iota(jnp.int32, (FRAMES, 128), 1) < HEAD

    def attend(pair, carry):
        cols = pl.ds(pl.multiple_of(pair * 128, 128), 128)
        both = query[:, cols]
        zero = jnp.zeros_like(both)
        stacked = jnp.concatenate(
            [jnp.where(lane_low, both, zero), jnp.where(lane_low, zero, both)], axis=0
        )
        scores = lax.dot_general(
            stacked, keys[:, cols], (((1,), (1,)), ((), ())), preferred_element_type=F32
        )
        mask = bias_mask[...]
        scores = scores + jnp.concatenate([mask, mask], axis=0)
        highest = jnp.max(scores, axis=1, keepdims=True)
        weight = jnp.exp(scores - highest)
        denominator = jnp.sum(weight, axis=1, keepdims=True)
        mixed = dot(weight.astype(BF16), values[:, cols]) / denominator
        context[:, cols] = jnp.where(lane_low, mixed[:FRAMES], mixed[FRAMES:]).astype(BF16)
        return carry

    lax.fori_loop(0, LOCAL // 128, attend, 0)

    def br_copy(n):
        return remote(br_out.at[n], br_in.at[n], br_send.at[n], br_recv.at[n], {"phase": other})

    for n in range(3):
        cols = pl.ds(pl.multiple_of(other * LOCAL + n * CUT, CUT), CUT)
        br_out[n] = dot(context[...], out_w[:, cols]).astype(BF16)
        br_copy(n).start()
    frames_copy.wait_recv()
    for n in range(3):
        cols = pl.ds(pl.multiple_of(phase * LOCAL + n * CUT, CUT), CUT)
        here = slice(n * CUT, (n + 1) * CUT)
        total = frames_cols[:, here].astype(F32) + dot(context[...], out_w[:, cols])
        br_copy(n).wait_recv()
        out_ref[:, here] = (total + br_in[n].astype(F32)).astype(BF16)

    halo_copy.wait_send()
    for copy in w_copies:
        copy.wait_send()

    def maps_sent(g, carry):
        for dx in range(1, SIDE):
            maps_copy(dx, g).wait_send()
        return carry

    lax.fori_loop(0, TILES, maps_sent, 0)

    def sums_sent(n, carry):
        sib_copy(n).wait_send()
        for dx in range(1, SIDE):
            rs_copy(dx, n).wait_send()
        return carry

    lax.fori_loop(0, CUTS, sums_sent, 0)
    frames_copy.wait_send()
    own_copy.wait_send()
    for k in range(len(NEAR)):
        near[k].wait_send()
        forward[k].wait_send()
    for n in range(3):
        br_copy(n).wait_send()


def local(
    features,
    lengths,
    conv1_weight,
    conv1_bias,
    conv2_weight,
    conv2_bias,
    proj_weight,
    proj_bias,
    norm_gain,
    qkv_weight,
    out_weight,
):
    vmem = pl.BlockSpec(memory_space=pltpu.VMEM)
    smem = pl.BlockSpec(memory_space=pltpu.SMEM)
    hbm = pl.BlockSpec(memory_space=pl.ANY)
    dma = pltpu.SemaphoreType.DMA
    scratch = [
        pltpu.VMEM((16, 128), BF16),
        pltpu.VMEM((PADDED, 128), F32),
        pltpu.VMEM((384, BINS * 32), BF16),
        pltpu.VMEM((32, 768), F32),
        pltpu.VMEM((4, 128, 768), BF16),
        pltpu.VMEM((TILES, ROWS, 128), BF16),
        pltpu.VMEM((768, 256), BF16),
        pltpu.VMEM((768, 128), BF16),
        pltpu.VMEM((4 * EVEN, 768), BF16),
        pltpu.VMEM((4 * FRAMES, 768), BF16),
        pltpu.VMEM((TILES, 128, WIDTH), BF16),
        pltpu.VMEM((SIDE, TILES, FRAMES, 128), BF16),
        pltpu.VMEM((SIDE, TILES, FRAMES, 128), BF16),
        pltpu.VMEM((CUTS, SIDE, FRAMES, CUT), F32),
        pltpu.VMEM((CUTS, SIDE, HALF, CUT), BF16),
        pltpu.VMEM((CUTS, SIDE, HALF, CUT), BF16),
        pltpu.VMEM((CUTS, SIDE, HALF, CUT), F32),
        pltpu.VMEM((CUTS, SIDE, HALF, CUT), BF16),
        pltpu.VMEM((SIDE - 1, CUTS, HALF, CUT), BF16),
        pltpu.VMEM((HALF, WIDTH), BF16),
        pltpu.VMEM((FRAMES, LOCAL), BF16),
        pltpu.VMEM((SPAN, WIDTH), BF16),
        pltpu.VMEM((3, WIDTH, LOCAL), BF16),
        pltpu.VMEM((LOCAL, WIDTH), BF16),
        pltpu.VMEM((FRAMES, LOCAL), BF16),
        pltpu.VMEM((SPAN, LOCAL), BF16),
        pltpu.VMEM((SPAN, LOCAL), BF16),
        pltpu.VMEM((FRAMES, SPAN), F32),
        pltpu.VMEM((FRAMES, LOCAL), BF16),
        pltpu.VMEM((3, FRAMES, CUT), BF16),
        pltpu.VMEM((3, FRAMES, CUT), BF16),
        dma((9,)),
        dma,
        dma,
        dma,
        dma,
        dma((3,)),
        dma((3,)),
        dma((3, TILES)),
        dma((3, TILES)),
        dma((CUTS,)),
        dma((CUTS,)),
        dma((3, CUTS)),
        dma((3, CUTS)),
        dma,
        dma,
        dma((4,)),
        dma((4,)),
        dma,
        dma,
        dma((4,)),
        dma((4,)),
        dma((3,)),
        dma((3,)),
    ]
    encoded = pl.pallas_call(
        body,
        out_shape=jax.ShapeDtypeStruct((FRAMES, LOCAL), BF16),
        in_specs=[smem, vmem, vmem, vmem, hbm, vmem, vmem, vmem, vmem, hbm, hbm],
        out_specs=vmem,
        scratch_shapes=scratch,
        compiler_params=pltpu.CompilerParams(
            collective_id=0, has_side_effects=True, vmem_limit_bytes=48 * 1024 * 1024
        ),
    )(
        lengths,
        features[0],
        conv1_weight,
        conv1_bias[None],
        conv2_weight,
        conv2_bias[None],
        proj_weight,
        proj_bias[None],
        norm_gain[None],
        qkv_weight.transpose(1, 0, 2),
        out_weight,
    )
    return encoded[None]


def solution(mesh):
    in_specs = (
        P("batch", "seq", None),
        P("batch", None),
        P(),
        P(),
        P(None, None, None, "phase"),
        P("phase"),
        P(("phase", "seq"), None),
        P(),
        P(),
        P(None, None, "phase"),
        P("phase", None),
    )
    out_specs = P("batch", "seq", "phase")
    return jax.shard_map(local, mesh=mesh, in_specs=in_specs, out_specs=out_specs, check_vma=False)
```

time: 241 us -> 94.6 us (0.39)
  Pallas kernels: 0 us -> 84.7 us
  waiting for transfers between devices: 74.1 us -> 0 us
  local copies, waits for them, and re-layouts: 62.9 us -> 9.54 us
  other arithmetic: 40.9 us -> 0 us
  matrix products: 33.2 us -> 0 us
  starting transfers between devices: 14.7 us -> 0 us
  between operations: 13.9 us -> 0.02 us
    pallas_call x0 -> x1, Pallas kernels: none -> 84.7 us  [local(): pl.pallas_call(body, out_shape=jax.ShapeDtypeStruct((FRAMES, LOCAL), BF16...]
    dot_general x22 -> x0, matrix products: 32 us -> none  [the longest x9 7.5 us: second_conv(): jnp.dot(tapped.reshape(frames_out * quarter, channels), weights[step_time...]
    slice x31 -> x0, local copies, waits for them, and re-layouts: 27.7 us -> none  [the longest x7 10.5 us: attend(): value_heads = piece[1].reshape(rows_here, heads_here, HEAD)]
    convert_element_type x3 -> x0, other arithmetic: 24.1 us -> none  [the longest x1 22 us: first_conv(): return jax.nn.relu(summed).astype(jnp.bfloat16)]
    all_gather x1 -> x0, waiting for transfers between devices: 24.1 us -> none  [local(): lax.all_gather(proj_weight, 'seq', axis=0, tiled=True)]
    psum x1 -> x0, waiting for transfers between devices: 20 us -> none  [local(): summed = lax.psum(partial_frames, 'phase')]
    reduce_scatter x1 -> x0, waiting for transfers between devices: 16.1 us -> none  [local(): lax.psum_scatter(branch.astype(jnp.bfloat16), 'phase', scatter_dimension=...]
    mul x18 -> x0, local copies, waits for them, and re-layouts: 15.4 us -> none  [first_conv(): summed = summed + tapped[:, :, None] * weights[step_time, step_bin]]
  transfers between devices with their start and end apart: 8 -> 0, of which waited for: 5 -> 0; matrix products, arithmetic and copies ran while one was open for 39% -> 0% of each run, Pallas kernels for 0% -> 0%
where the time goes in v1:
time: 94.6 us; the launch traced here: 94.2 us
  Pallas kernels  84.7 us (90%)
  local copies, waits for them, and re-layouts  9.54 us (10%)
    pallas_call x1, Pallas kernels, local(): pl.pallas_call(body, out_shape=jax.ShapeDtypeStruct((FRAMES, LOCAL), BF16...  84.7 us
    unnamed x17, local copies, waits for them, and re-layouts  8.14 us

profile of v1, /device:TPU:1, one launch (start us, length us, event | category | flops | bytes accessed | tf_op | source)
XLA Modules:
  0.0 94.2 jit_solution(2103521147548495500)
XLA Ops:
  0.0 0.7 broadcast_in_dim.17.pb_ref
  0.7 0.7 broadcast_in_dim.18.gain_ref
  1.4 0.0 copy-start
  1.4 1.7 %copy-done = bf16[768,1536]{1,0:T(8,128)(2,1)S(1)} copy-done((bf16[768,1536]{1,0:T(8,128)(2,1)S(1)}, bf16[768,1536]{1,0:T(8,128)(2,1)}, u32[]{:S(2)}) %copy-start) | copy-done | bytes 2359320
  3.1 0.0 copy-start.1
  3.1 1.1 %copy-done.1 = bf16[256,1536]{1,0:T(8,128)(2,1)S(1)} copy-done((bf16[256,1536]{1,0:T(8,128)(2,1)S(1)}, bf16[256,1536]{1,0:T(8,128)(2,1)}, u32[]{:S(2)}) %copy-start.1) | copy-done | bytes 786456
  4.2 0.0 copy-start.2
  4.2 1.1 %copy-done.2 = bf16[3,3,256,128]{3,2,1,0:T(8,128)(2,1)S(1)} copy-done((bf16[3,3,256,128]{3,2,1,0:T(8,128)(2,1)S(1)}, bf16[3,3,256,128]{3,2,1,0:T(8,128)(2,1)}, u32[]{:S(2)}) %copy-start.2) | copy-done | bytes 589848
  5.3 0.0 copy-start.3
  5.3 0.9 copy-done.3
  6.2 0.0 copy-start.4
  6.2 0.7 copy-done.4
  6.9 0.0 copy-start.5
  6.9 0.7 copy-done.5
  7.6 0.0 copy-start.6
  7.6 0.7 copy-done.6
  8.2 0.0 copy-start.7
  8.2 0.7 copy-done.7
  8.9 84.7 %shard_map.109 = bf16[128,768]{1,0:T(8,128)(2,1)S(1)} custom-call(s32[1,12]{1,0:T(1,128)S(1)} %copy-done.6, bf16[512,128]{1,0:T(8,128)(2,1)S(1)} %bitcast.6, f32[3,3,256]{2,1,0:T(4,128)S(1)} %copy-done.4, f32[1,256]{1,0:T(1,128)S(1)} %bitcast.7, bf16[3,3,256,128]{3,2,1,0:T(8,128)(2,1)S(1)} %copy-done.2, f32[1,128]{1,0:T(1,128)S(1)} %bitcast.8, ...), custom_call_target="tpu_custom_call" | custom-call | tf_op jit(solution)/shard_map/pallas_call | solution.py:589
  93.5 0.7 copy.13
Async XLA Ops:
  1.4 1.7 %copy-start = (bf16[768,1536]{1,0:T(8,128)(2,1)S(1)}, bf16[768,1536]{1,0:T(8,128)(2,1)}, u32[]{:S(2)}) copy-start(bf16[768,1536]{1,0:T(8,128)(2,1)} %wo_ref.1) | copy-start | bytes 7077892
  3.1 1.1 %copy-start.1 = (bf16[256,1536]{1,0:T(8,128)(2,1)S(1)}, bf16[256,1536]{1,0:T(8,128)(2,1)}, u32[]{:S(2)}) copy-start(bf16[256,1536]{1,0:T(8,128)(2,1)} %wp_ref.1) | copy-start | bytes 2359300
  4.2 1.1 %copy-start.2 = (bf16[3,3,256,128]{3,2,1,0:T(8,128)(2,1)S(1)}, bf16[3,3,256,128]{3,2,1,0:T(8,128)(2,1)}, u32[]{:S(2)}) copy-start(bf16[3,3,256,128]{3,2,1,0:T(8,128)(2,1)} %w2_ref.1) | copy-start | bytes 1769476
  5.3 0.9 copy-start.3
  6.2 0.7 copy-start.4
  6.9 0.7 copy-start.5
  7.6 0.7 copy-start.6
  8.2 0.7 copy-start.7

commit v2 on v1

--- a/solution.py
+++ b/solution.py
@@ -2,7 +2,6 @@
 
 import jax
 import jax.numpy as jnp
-import numpy as np
 from jax import lax
 from jax.experimental import pallas as pl
 from jax.experimental.pallas import tpu as pltpu
@@ -16,6 +15,7 @@
 BLOCKS = SIDE * SIDE
 FRAMES = 128
 HALF = 64
+QUARTER = 32
 BINS = 32
 UTTS = 12
 WIDTH = 1536
@@ -38,17 +38,24 @@
 
 def body(
     lengths_ref,
+    feat_hbm,
+    w1_hbm,
+    b1_hbm,
+    w2_ref,
+    b2_hbm,
+    wp_hbm,
+    pb_hbm,
+    gain_hbm,
+    qkv_ref,
+    wo_ref,
+    out_ref,
     feat_ref,
     w1_ref,
     b1_ref,
-    w2_ref,
     b2_ref,
     wp_ref,
     pb_ref,
     gain_ref,
-    qkv_ref,
-    wo_ref,
-    out_ref,
     halo,
     padded,
     picker,
@@ -57,8 +64,8 @@
     patches,
     w2_even,
     w2_odd,
-    fe,
-    fo,
+    first_even,
+    first_odd,
     w_all,
     maps_out,
     maps_in,
@@ -80,13 +87,16 @@
     context,
     br_out,
     br_in,
+    in_sem,
     w2_sem,
     qkv_sem,
     out_sem,
     halo_send,
     halo_recv,
-    w_send,
-    w_recv,
+    wy_send,
+    wy_recv,
+    wz_send,
+    wz_recv,
     m_send,
     m_recv,
     sib_send,
@@ -97,10 +107,8 @@
     fr_recv,
     n_send,
     n_recv,
-    own_send,
-    own_recv,
-    fw_send,
-    fw_recv,
+    s_send,
+    s_recv,
     br_send,
     br_recv,
 ):
@@ -108,13 +116,21 @@
     block = lax.axis_index("seq")
     x = block % SIDE
     y = block // SIDE
+    plane = lax.axis_index("batch")
+    planes = lax.axis_size("batch")
     other = 1 - phase
+
+    def row_of(ref):
+        return jnp.concatenate([ref[k : k + 1, :] for k in range(WIDTH // 128)], axis=1)
 
     def row_peer(dx):
         return y * SIDE + (x + dx) % SIDE
 
     def column_peer(dy):
-        return ((y + dy) % SIDE) * SIDE + x
+        return ((y + dy + SIDE) % SIDE) * SIDE + x
+
+    def plane_peer(dz):
+        return (plane + dz + planes) % planes
 
     def near_peer(d):
         return (block + d + BLOCKS) % BLOCKS
@@ -129,6 +145,22 @@
             device_id_type=MESH,
         )
 
+    inputs = [
+        pltpu.make_async_copy(source, target, in_sem.at[k])
+        for k, (source, target) in enumerate(
+            (
+                (wp_hbm, wp_ref),
+                (feat_hbm, feat_ref),
+                (w1_hbm, w1_ref),
+                (b1_hbm, b1_ref),
+                (b2_hbm, b2_ref),
+                (pb_hbm, pb_ref),
+                (gain_hbm, gain_ref),
+            )
+        )
+    ]
+    for copy in inputs:
+        copy.start()
     local_w2 = []
     for b in range(3):
         rows = pl.ds(b * 256, 256)
@@ -151,8 +183,9 @@
     barrier = pltpu.get_barrier_semaphore()
     peers = [{"phase": other}]
     peers += [{"seq": row_peer(dx)} for dx in range(1, SIDE)]
-    peers += [{"seq": column_peer(dy)} for dy in range(1, SIDE)]
-    peers += [{"seq": near_peer(d)} for d in NEAR]
+    peers += [{"seq": column_peer(dy)} for dy in (1, 3)]
+    peers += [{"batch": plane_peer(dz)} for dz in (1, -1)]
+    peers += [{"seq": near_peer(d)} for d in (1, -1)]
     for peer in peers:
         pl.semaphore_signal(barrier, inc=1, device_id=peer, device_id_type=MESH)
 
@@ -160,31 +193,63 @@
     in_row = lax.broadcasted_iota(jnp.int32, (256, 256), 1)
     reorder = jnp.where(in_row == (out_row & 7) * BINS + (out_row >> 3), 1.0, 0.0).astype(BF16)
     own_rows = pl.ds(pl.multiple_of(y * 32, 32), 32)
+    inputs[0].wait()
     for n in range(CUTS):
         cols = slice(n * CUT, (n + 1) * CUT)
         moved = dot(reorder, wp_ref[:, cols]).astype(BF16)
         for g in range(TILES):
             w_all[g, own_rows, cols] = moved[g * 32 : (g + 1) * 32]
 
+    inputs[1].wait()
     pl.semaphore_wait(barrier, len(peers))
 
     halo_copy = remote(
         feat_ref.at[pl.ds(496, 16)], halo, halo_send, halo_recv, {"seq": near_peer(1)}
     )
     halo_copy.start()
-    w_copies = []
-    for dy in range(1, SIDE):
-        w_copies.append(
-            remote(
-                w_all.at[:, own_rows, :],
-                w_all.at[:, own_rows, :],
-                w_send.at[dy - 1],
-                w_recv.at[dy - 1],
-                {"seq": column_peer(dy)},
-            )
-        )
-    for k in (0, 2, 1):
-        w_copies[k].start()
+    drain = [halo_copy.wait_send]
+    half_low = (plane % 2) * 4
+    pieces = [
+        (-1, 0, 1),
+        (1, 1, -1),
+        (-1, 1, -1),
+        (1, 0, 1),
+        (2, 0, 1),
+        (2, 1, -1),
+    ]
+
+    def w_piece(dy, part_of, low):
+        rows = pl.ds(pl.multiple_of(((y + dy + SIDE) % SIDE) * 32, 32), 32)
+        return w_all.at[pl.ds(low + 2 * part_of, 2), rows, :]
+
+    def w_along_y(k):
+        dy, part_of, _ = pieces[k]
+        step = -1 if dy == -1 or (dy == 2 and part_of == 0) else 1
+        mine = w_piece(dy - step, part_of, half_low)
+        return remote(
+            mine, mine, wy_send.at[k], wy_recv.at[k], {"seq": column_peer(-step)}
+        )
+
+    def w_along_z(k):
+        dy, part_of, dz = pieces[k]
+        mine = w_piece(dy, part_of, half_low)
+        return remote(mine, mine, wz_send.at[k], wz_recv.at[k], {"batch": plane_peer(dz)})
+
+    def w_sent():
+        for k in range(6):
+            w_along_y(k).wait_send()
+            w_along_z(k).wait_send()
+
+    drain.append(w_sent)
+    for k in range(4):
+        w_along_y(k).start()
+
+    def w_step(step):
+        for k in (2 * step, 2 * step + 1):
+            w_along_y(k).wait_recv()
+            if step == 0:
+                w_along_y(4 + k).start()
+            w_along_z(k).start()
 
     offsets = []
     running = jnp.int32(0)
@@ -207,35 +272,39 @@
         cols = slice(j * 128, (j + 1) * 128)
         bias_mask[:, cols] = jnp.where(seg_query == seg_key[0:1, cols], 0.0, -1e30)
 
+    for copy in inputs[2:]:
+        copy.wait()
     base[...] = jnp.zeros_like(base)
+
+    def two_pieces(value):
+        high = value.astype(BF16).astype(F32)
+        return high, value - high
+
     for a in range(3):
+        pair = two_pieces(w1_ref[a])
         for b in range(3):
-            for shift in range(3):
-                row = 8 * a + 2 * shift + b
-                base[row : row + 1, shift * 256 : (shift + 1) * 256] = w1_ref[a, b : b + 1, :]
-    bias1 = b1_ref[...]
-    high = bias1.astype(BF16).astype(F32)
-    middle = (bias1 - high).astype(BF16).astype(F32)
-    for k, piece in enumerate((high, middle, bias1 - high - middle)):
-        base[24 + k : 25 + k, 0:256] = piece
-        base[8 * k + 7 : 8 * k + 8, 256:512] = piece
-        base[8 * k + 7 : 8 * k + 8, 512:768] = piece
+            for shift in range(2):
+                for k in range(2):
+                    row = 15 * k + 5 * a + 2 * shift + b
+                    base[row : row + 1, shift * 256 : (shift + 1) * 256] = pair[k][b : b + 1, :]
+    pair = two_pieces(jnp.concatenate([b1_ref[0:1, :], b1_ref[1:2, :]], axis=1))
+    for k in range(2):
+        for shift in range(2):
+            base[30 + k : 31 + k, shift * 256 : (shift + 1) * 256] = pair[k]
     taps[...] = jnp.zeros_like(taps)
     for r in range(4):
         taps[r, 32 * r : 32 * r + 32, :] = base[...].astype(BF16)
 
-    bins_in = lax.broadcasted_iota(jnp.int32, (128, BINS * 32), 0)
-    lane = lax.broadcasted_iota(jnp.int32, (128, BINS * 32), 1)
-    tap_bin = lane & 7
-    tap_time = (lane >> 3) & 3
-    hit = (bins_in == ((lane >> 5) * 4 + tap_bin - 3)) & (tap_bin < 7)
+    lane = lax.broadcasted_iota(jnp.int32, (1, BINS * 32), 1)
+    low = lane & 31
+    tap = jnp.where(low >= 15, low - 15, low)
+    tap_time = jnp.where(tap >= 5, 1, 0) + jnp.where(tap >= 10, 1, 0)
+    tap_bin = (lane >> 5) * 4 + (tap - 5 * tap_time) - 1
+    wanted = jnp.where((low < 30) & (tap_bin >= 0), tap_time * 128 + tap_bin, -1)
+    constant = jnp.where(low >= 30, 1.0, 0.0)
     for a in range(3):
-        picker[a * 128 : (a + 1) * 128, :] = jnp.where(hit & (tap_time == a), 1.0, 0.0).astype(BF16)
-    lane1 = lax.broadcasted_iota(jnp.int32, (1, BINS * 32), 1)
-    low = lane1 & 31
-    constant = ((low & 7) == 7) & (low < 24)
-    constant = constant | ((low >= 24) & (low < 27) & (lane1 >= 32))
-    constant = jnp.where(constant, 1.0, 0.0)
+        bins_in = lax.broadcasted_iota(jnp.int32, (128, BINS * 32), 0) + a * 128
+        picker[a * 128 : (a + 1) * 128, :] = jnp.where(bins_in == wanted, 1.0, 0.0).astype(BF16)
 
     padded[8:520, :] = feat_ref[...].astype(F32)
     padded[520:PADDED, :] = jnp.zeros((PADDED - 520, 128), F32)
@@ -271,19 +340,30 @@
 
     def convolve(g, carry):
         patch = patches[g]
+        first_odd[0] = first_odd[4]
         for r in range(4):
-            for shift in range(3):
-                cols = slice(shift * 256, (shift + 1) * 256)
-                first_map = jnp.maximum(dot(patch, taps[r, :, cols]), 0.0).astype(BF16)
-                fe[r * EVEN : (r + 1) * EVEN, cols] = first_map[:EVEN]
-                fo[r * FRAMES : (r + 1) * FRAMES, cols] = first_map[EVEN:]
+            first_even[r] = jnp.maximum(dot(patch, taps[r, :, 0:256]), 0.0).astype(BF16)
+            first_odd[r + 1] = jnp.maximum(dot(patch, taps[r, :, 256:512]), 0.0).astype(BF16)
+
+        def three_bins(rows):
+            return jnp.concatenate(
+                [
+                    jnp.concatenate(
+                        [first_odd[r, rows], first_even[r, rows], first_odd[r + 1, rows]], axis=1
+                    )
+                    for r in range(4)
+                ],
+                axis=0,
+            )
+
+        sums = dot(three_bins(slice(0, EVEN)), w2_even[...])
+        sums_odd = dot(three_bins(slice(EVEN, ROWS)), w2_odd[...])
         second = []
         for r in range(4):
-            sums = dot(fe[r * EVEN : (r + 1) * EVEN, :], w2_even[...])
-            sums_odd = dot(fo[r * FRAMES : (r + 1) * FRAMES, :], w2_odd[...])
-            later = pltpu.roll(sums[:, 128:256], EVEN - 1, 0)[:FRAMES]
-            total = sums[:FRAMES, 0:128] * kept + later + sums_odd + bias2
-            second.append(jnp.maximum(total, 0.0))
+            here = sums[r * EVEN : (r + 1) * EVEN]
+            later = pltpu.roll(here[:, 128:256], EVEN - 1, 0)[:FRAMES]
+            total = here[:FRAMES, 0:128] * kept + later + sums_odd[r * FRAMES : (r + 1) * FRAMES]
+            second.append(jnp.maximum(total + bias2, 0.0))
         for to in range(SIDE):
             mixed = second[to]
             for r in range(4):
@@ -293,9 +373,22 @@
             maps_out[to, g] = mixed.astype(BF16)
         for dx in (2, 1, 3):
             maps_copy(dx, g).start()
+        for step, at in ((0, 0), (1, 4)):
+            pl.when(g == at)(lambda step=step: w_step(step))
         return carry
 
+    def maps_sent():
+        def step(g, carry):
+            for dx in range(1, SIDE):
+                maps_copy(dx, g).wait_send()
+            return carry
+
+        lax.fori_loop(0, TILES, step, 0)
+
+    drain.append(maps_sent)
+    first_odd[4] = jnp.zeros((ROWS, 256), BF16)
     lax.fori_loop(0, TILES, convolve, 0)
+    w_step(2)
 
     for g in range(TILES):
         maps_in[x, g] = maps_out[x, g]
@@ -306,8 +399,8 @@
         return carry
 
     lax.fori_loop(0, TILES, maps_wait, 0)
-    for copy in w_copies:
-        copy.wait_recv()
+    for k in range(6):
+        w_along_z(k).wait_recv()
 
     mine = pl.ds(pl.multiple_of(phase * HALF, HALF), HALF)
     theirs = pl.ds(pl.multiple_of(other * HALF, HALF), HALF)
@@ -359,8 +452,19 @@
 
         return carry
 
+    def sums_sent():
+        def step(n, carry):
+            sib_copy(n).wait_send()
+            for dx in range(1, SIDE):
+                rs_copy(dx, n).wait_send()
+            return carry
+
+        lax.fori_loop(0, CUTS, step, 0)
+
+    drain.append(sums_sent)
     lax.fori_loop(0, CUTS + 2, project_step, 0)
 
+    proj_bias = row_of(pb_ref)
     for n in range(CUTS):
         cols = slice(n * CUT, (n + 1) * CUT)
         for dx in range(1, SIDE):
@@ -368,7 +472,7 @@
         total = tot[n, x]
         for dx in range(1, SIDE):
             total = total + rs_in[dx - 1, n].astype(F32)
-        frames_mine[:, cols] = (total + pb_ref[:, cols]).astype(BF16)
+        frames_mine[:, cols] = (total + proj_bias[:, cols]).astype(BF16)
     frames_copy = remote(
         frames_mine.at[:, pl.ds(pl.multiple_of(other * LOCAL, LOCAL), LOCAL)],
         frames_cols.at[mine, :],
@@ -377,47 +481,48 @@
         {"phase": other},
     )
     frames_copy.start()
+    drain.append(frames_copy.wait_send)
     numbers = frames_mine[...].astype(F32)
     average = jnp.mean(numbers, axis=1, keepdims=True)
     centered = numbers - average
     variance = jnp.mean(centered * centered, axis=1, keepdims=True)
     own_slot = pl.ds(pl.multiple_of(REACH * FRAMES + phase * HALF, HALF), HALF)
-    normed[own_slot, :] = (centered * lax.rsqrt(variance + 1e-05) * gain_ref[...]).astype(BF16)
-
-    def slot(d):
-        return pl.ds(pl.multiple_of((REACH + d) * FRAMES + phase * HALF, HALF), HALF)
-
-    near = []
-    forward = []
-    for k, d in enumerate(NEAR):
-        near.append(
-            remote(
-                normed.at[own_slot, :],
-                normed.at[slot(d), :],
-                n_send.at[k],
-                n_recv.at[k],
-                {"seq": near_peer(-d)},
-            )
-        )
-        forward.append(
-            remote(
-                normed.at[slot(d), :],
-                normed.at[slot(d), :],
-                fw_send.at[k],
-                fw_recv.at[k],
-                {"phase": other},
-            )
-        )
-    own_copy = remote(
-        normed.at[own_slot, :], normed.at[own_slot, :], own_send, own_recv, {"phase": other}
-    )
-    for k in (0, 3, 1, 2):
-        near[k].start()
-    own_copy.start()
+    normed[own_slot, :] = (centered * lax.rsqrt(variance + 1e-05) * row_of(gain_ref)).astype(BF16)
+
+    def slot(d, k):
+        return pl.ds(
+            pl.multiple_of((REACH + d) * FRAMES + phase * HALF + k * QUARTER, QUARTER), QUARTER
+        )
+
+    def near_copy(d, k):
+        step = 1 if d > 0 else -1
+        source = normed.at[slot(d - step, k), :]
+        target = normed.at[slot(d, k), :]
+        sem = (NEAR.index(d), k)
+        return remote(source, target, n_send.at[sem], n_recv.at[sem], {"seq": near_peer(-step)})
+
+    def share_copy(d, k):
+        rows = normed.at[slot(d, k), :]
+        sem = (d + REACH, k)
+        return remote(rows, rows, s_send.at[sem], s_recv.at[sem], {"phase": other})
+
+    def near_sent():
+        for k in range(2):
+            for d in NEAR:
+                near_copy(d, k).wait_send()
+            for d in range(-REACH, REACH + 1):
+                share_copy(d, k).wait_send()
+
+    drain.append(near_sent)
+    for k in range(2):
+        for d in (-1, 1):
+            near_copy(d, k).start()
+        share_copy(0, k).start()
     frames_cols[mine, :] = frames_mine[:, pl.ds(pl.multiple_of(phase * LOCAL, LOCAL), LOCAL)]
     qkv_copy.wait()
     out_copy.wait()
-    own_copy.wait_recv()
+    for k in range(2):
+        share_copy(0, k).wait_recv()
 
     def keys_values(low, rows):
         block_rows = normed[low : low + rows, :]
@@ -433,20 +538,17 @@
         made = dot(own_block, qkv_w[0, :, cols]).astype(BF16)
         query[:, cols] = made * jnp.asarray(1.0 / math.sqrt(HEAD), BF16)
     keys_values(own_low, FRAMES)
-    for k in (1, 2):
-        near[k].wait_recv()
-        forward[k].start()
-    for k in (1, 2):
-        forward[k].wait_recv()
-    keys_values(FRAMES, FRAMES)
-    keys_values(3 * FRAMES, FRAMES)
-    for k in (0, 3):
-        near[k].wait_recv()
-        forward[k].start()
-    for k in (0, 3):
-        forward[k].wait_recv()
-    keys_values(0, FRAMES)
-    keys_values(4 * FRAMES, FRAMES)
+    for distance in (1, 2):
+        for k in range(2):
+            for d in (-distance, distance):
+                near_copy(d, k).wait_recv()
+                if distance == 1:
+                    near_copy(2 * d, k).start()
+                share_copy(d, k).start()
+        for d in (-distance, distance):
+            for k in range(2):
+                share_copy(d, k).wait_recv()
+            keys_values((REACH + d) * FRAMES, FRAMES)
 
     lane_low = lax.broadcasted_iota(jnp.int32, (FRAMES, 128), 1) < HEAD
 
@@ -478,6 +580,7 @@
         cols = pl.ds(pl.multiple_of(other * LOCAL + n * CUT, CUT), CUT)
         br_out[n] = dot(context[...], out_w[:, cols]).astype(BF16)
         br_copy(n).start()
+        drain.append(br_copy(n).wait_send)
     frames_copy.wait_recv()
     for n in range(3):
         cols = pl.ds(pl.multiple_of(phase * LOCAL + n * CUT, CUT), CUT)
@@ -486,31 +589,8 @@
         br_copy(n).wait_recv()
         out_ref[:, here] = (total + br_in[n].astype(F32)).astype(BF16)
 
-    halo_copy.wait_send()
-    for copy in w_copies:
-        copy.wait_send()
-
-    def maps_sent(g, carry):
-        for dx in range(1, SIDE):
-            maps_copy(dx, g).wait_send()
-        return carry
-
-    lax.fori_loop(0, TILES, maps_sent, 0)
-
-    def sums_sent(n, carry):
-        sib_copy(n).wait_send()
-        for dx in range(1, SIDE):
-            rs_copy(dx, n).wait_send()
-        return carry
-
-    lax.fori_loop(0, CUTS, sums_sent, 0)
-    frames_copy.wait_send()
-    own_copy.wait_send()
-    for k in range(len(NEAR)):
-        near[k].wait_send()
-        forward[k].wait_send()
-    for n in range(3):
-        br_copy(n).wait_send()
+    for wait in drain:
+        wait()
 
 
 def local(
@@ -531,16 +611,23 @@
     hbm = pl.BlockSpec(memory_space=pl.ANY)
     dma = pltpu.SemaphoreType.DMA
     scratch = [
+        pltpu.VMEM((4 * FRAMES, 128), BF16),
+        pltpu.VMEM((3, 3, 256), F32),
+        pltpu.VMEM((2, 128), F32),
+        pltpu.VMEM((1, 128), F32),
+        pltpu.VMEM((256, WIDTH), BF16),
+        pltpu.VMEM((WIDTH // 128, 128), F32),
+        pltpu.VMEM((WIDTH // 128, 128), F32),
         pltpu.VMEM((16, 128), BF16),
         pltpu.VMEM((PADDED, 128), F32),
         pltpu.VMEM((384, BINS * 32), BF16),
-        pltpu.VMEM((32, 768), F32),
-        pltpu.VMEM((4, 128, 768), BF16),
+        pltpu.VMEM((32, 512), F32),
+        pltpu.VMEM((4, 128, 512), BF16),
         pltpu.VMEM((TILES, ROWS, 128), BF16),
         pltpu.VMEM((768, 256), BF16),
         pltpu.VMEM((768, 128), BF16),
-        pltpu.VMEM((4 * EVEN, 768), BF16),
-        pltpu.VMEM((4 * FRAMES, 768), BF16),
+        pltpu.VMEM((4, ROWS, 256), BF16),
+        pltpu.VMEM((5, ROWS, 256), BF16),
         pltpu.VMEM((TILES, 128, WIDTH), BF16),
         pltpu.VMEM((SIDE, TILES, FRAMES, 128), BF16),
         pltpu.VMEM((SIDE, TILES, FRAMES, 128), BF16),
@@ -562,13 +649,16 @@
         pltpu.VMEM((FRAMES, LOCAL), BF16),
         pltpu.VMEM((3, FRAMES, CUT), BF16),
         pltpu.VMEM((3, FRAMES, CUT), BF16),
+        dma((7,)),
         dma((9,)),
         dma,
         dma,
         dma,
         dma,
-        dma((3,)),
-        dma((3,)),
+        dma((6,)),
+        dma((6,)),
+        dma((6,)),
+        dma((6,)),
         dma((3, TILES)),
         dma((3, TILES)),
         dma((CUTS,)),
@@ -577,34 +667,32 @@
         dma((3, CUTS)),
         dma,
         dma,
-        dma((4,)),
-        dma((4,)),
-        dma,
-        dma,
-        dma((4,)),
-        dma((4,)),
+        dma((4, 2)),
+        dma((4, 2)),
+        dma((5, 2)),
+        dma((5, 2)),
         dma((3,)),
         dma((3,)),
     ]
     encoded = pl.pallas_call(
         body,
         out_shape=jax.ShapeDtypeStruct((FRAMES, LOCAL), BF16),
-        in_specs=[smem, vmem, vmem, vmem, hbm, vmem, vmem, vmem, vmem, hbm, hbm],
+        in_specs=[smem] + [hbm] * 10,
         out_specs=vmem,
         scratch_shapes=scratch,
         compiler_params=pltpu.CompilerParams(
-            collective_id=0, has_side_effects=True, vmem_limit_bytes=48 * 1024 * 1024
+            collective_id=0, has_side_effects=True, vmem_limit_bytes=60 * 1024 * 1024
         ),
     )(
         lengths,
         features[0],
         conv1_weight,
-        conv1_bias[None],
+        conv1_bias.reshape(2, 128),
         conv2_weight,
         conv2_bias[None],
         proj_weight,
-        proj_bias[None],
-        norm_gain[None],
+        proj_bias.reshape(WIDTH // 128, 128),
+        norm_gain.reshape(WIDTH // 128, 128),
         qkv_weight.transpose(1, 0, 2),
         out_weight,
     )

time: 94.6 us -> 68.6 us (0.73)
  Pallas kernels: 84.7 us -> 66.9 us
  local copies, waits for them, and re-layouts: 9.54 us -> 1.62 us
    pallas_call x1, Pallas kernels: 84.7 us -> 66.9 us  [local(): pl.pallas_call(body, out_shape=jax.ShapeDtypeStruct((FRAMES, LOCAL), BF16...]
    unnamed x17 -> x1, local copies, waits for them, and re-layouts: 8.14 us -> 1.62 us
    broadcast_in_dim x2 -> x0, local copies, waits for them, and re-layouts: 1.4 us -> none  [the longest x1 0.7 us: local(): proj_bias[None]]
where the time goes in v2:
time: 68.6 us; the launch traced here: 68.5 us
  Pallas kernels  66.9 us (98%)
  local copies, waits for them, and re-layouts  1.62 us (2%)
    pallas_call x1, Pallas kernels, local(): pl.pallas_call(body, out_shape=jax.ShapeDtypeStruct((FRAMES, LOCAL), BF16...  66.9 us
    unnamed x1, local copies, waits for them, and re-layouts  1.62 us

profile of v2, /device:TPU:1, one launch (start us, length us, event | category | flops | bytes accessed | tf_op | source)
XLA Modules:
  0.0 68.5 jit_solution(7499371082734754200)
XLA Ops:
  0.0 66.9 %shard_map.109 = bf16[128,768]{1,0:T(8,128)(2,1)} custom-call(s32[1,12]{1,0:T(1,128)} %lengths_ref.1, bf16[512,128]{1,0:T(8,128)(2,1)} %bitcast.9, f32[3,3,256]{2,1,0:T(4,128)} %w1_hbm.1, f32[2,128]{1,0:T(2,128)} %bitcast.12, bf16[3,3,256,128]{3,2,1,0:T(8,128)(2,1)} %w2_ref.1, f32[1,128]{1,0:T(1,128)} %bitcast.13, bf16[256,1536]{1,0:T(8,128)(2,1)} %wp_hbm.1, ...), custom_call_target="tpu_custom_call" | custom-call | tf_op jit(solution)/shard_map/pallas_call | solution.py:677
  66.9 1.6 %copy.13 = bf16[1,128,768]{2,1,0:T(8,128)(2,1)} copy(bf16[1,128,768]{2,1,0:T(8,128)(2,1)} %bitcast.8) | data formatting | bytes 393216

commit v3 on v2

--- a/solution.py
+++ b/solution.py
@@ -64,8 +64,10 @@
     patches,
     w2_even,
     w2_odd,
-    first_even,
-    first_odd,
+    even_a,
+    odd_a,
+    even_b,
+    odd_b,
     w_all,
     maps_out,
     maps_in,
@@ -84,6 +86,9 @@
     keys,
     values,
     bias_mask,
+    highest_mid,
+    denominator_mid,
+    numerator_mid,
     context,
     br_out,
     br_in,
@@ -338,19 +343,18 @@
             {"seq": row_peer(dx)},
         )
 
-    def convolve(g, carry):
+    def first_convolution(g, evens, odds, last_odds):
         patch = patches[g]
-        first_odd[0] = first_odd[4]
+        odds[0] = last_odds[4]
         for r in range(4):
-            first_even[r] = jnp.maximum(dot(patch, taps[r, :, 0:256]), 0.0).astype(BF16)
-            first_odd[r + 1] = jnp.maximum(dot(patch, taps[r, :, 256:512]), 0.0).astype(BF16)
-
+            evens[r] = jnp.maximum(dot(patch, taps[r, :, 0:256]), 0.0).astype(BF16)
+            odds[r + 1] = jnp.maximum(dot(patch, taps[r, :, 256:512]), 0.0).astype(BF16)
+
+    def second_convolution(g, evens, odds):
         def three_bins(rows):
             return jnp.concatenate(
                 [
-                    jnp.concatenate(
-                        [first_odd[r, rows], first_even[r, rows], first_odd[r + 1, rows]], axis=1
-                    )
+                    jnp.concatenate([odds[r, rows], evens[r, rows], odds[r + 1, rows]], axis=1)
                     for r in range(4)
                 ],
                 axis=0,
@@ -373,8 +377,15 @@
             maps_out[to, g] = mixed.astype(BF16)
         for dx in (2, 1, 3):
             maps_copy(dx, g).start()
-        for step, at in ((0, 0), (1, 4)):
-            pl.when(g == at)(lambda step=step: w_step(step))
+
+    def convolve(pair, carry):
+        g = 2 * pair
+        first_convolution(g + 1, even_b, odd_b, odd_a)
+        second_convolution(g, even_a, odd_a)
+        first_convolution(g + 2, even_a, odd_a, odd_b)
+        second_convolution(g + 1, even_b, odd_b)
+        for step, at in ((1, 0), (2, 2)):
+            pl.when(pair == at)(lambda step=step: w_step(step))
         return carry
 
     def maps_sent():
@@ -386,9 +397,13 @@
         lax.fori_loop(0, TILES, step, 0)
 
     drain.append(maps_sent)
-    first_odd[4] = jnp.zeros((ROWS, 256), BF16)
-    lax.fori_loop(0, TILES, convolve, 0)
-    w_step(2)
+    odd_b[4] = jnp.zeros((ROWS, 256), BF16)
+    first_convolution(0, even_a, odd_a, odd_b)
+    w_step(0)
+    lax.fori_loop(0, TILES // 2 - 1, convolve, 0)
+    first_convolution(TILES - 1, even_b, odd_b, odd_a)
+    second_convolution(TILES - 2, even_a, odd_a)
+    second_convolution(TILES - 1, even_b, odd_b)
 
     for g in range(TILES):
         maps_in[x, g] = maps_out[x, g]
@@ -399,9 +414,6 @@
         return carry
 
     lax.fori_loop(0, TILES, maps_wait, 0)
-    for k in range(6):
-        w_along_z(k).wait_recv()
-
     mine = pl.ds(pl.multiple_of(phase * HALF, HALF), HALF)
     theirs = pl.ds(pl.multiple_of(other * HALF, HALF), HALF)
 
@@ -419,17 +431,28 @@
             {"seq": row_peer(dx)},
         )
 
-    def project(n):
+    def half_sums(n, low):
         cols = pl.ds(pl.multiple_of(n * CUT, CUT), CUT)
         maps = jnp.concatenate(
             [
-                jnp.concatenate([maps_in[s, g] for g in range(TILES)], axis=1)
+                jnp.concatenate([maps_in[s, low + g] for g in range(4)], axis=1)
                 for s in range(SIDE)
             ],
             axis=0,
         )
-        weights = w_all[:, :, cols].reshape(TILES * 128, CUT)
-        part[n] = dot(maps, weights).reshape(SIDE, FRAMES, CUT)
+        weights = w_all[pl.ds(low, 4), :, cols].reshape(4 * 128, CUT)
+        return dot(maps, weights).reshape(SIDE, FRAMES, CUT)
+
+    def early(n, carry):
+        part[n] = half_sums(n, half_low)
+        return carry
+
+    lax.fori_loop(0, CUTS, early, 0)
+    for k in range(6):
+        w_along_z(k).wait_recv()
+
+    def project(n):
+        part[n] += half_sums(n, 4 - half_low)
         sib_out[n] = part[n, :, theirs, :].astype(BF16)
         sib_copy(n).start()
 
@@ -524,12 +547,14 @@
     for k in range(2):
         share_copy(0, k).wait_recv()
 
-    def keys_values(low, rows):
-        block_rows = normed[low : low + rows, :]
+    def keys_values(lows):
+        block_rows = jnp.concatenate([normed[low : low + FRAMES, :] for low in lows], axis=0)
         for n in range(3):
             cols = slice(n * CUT, (n + 1) * CUT)
-            keys[low : low + rows, cols] = dot(block_rows, qkv_w[1, :, cols]).astype(BF16)
-            values[low : low + rows, cols] = dot(block_rows, qkv_w[2, :, cols]).astype(BF16)
+            for j, target in ((1, keys), (2, values)):
+                made = dot(block_rows, qkv_w[j, :, cols]).astype(BF16)
+                for i, low in enumerate(lows):
+                    target[low : low + FRAMES, cols] = made[i * FRAMES : (i + 1) * FRAMES]
 
     own_low = REACH * FRAMES
     own_block = normed[own_low : own_low + FRAMES, :]
@@ -537,41 +562,69 @@
         cols = slice(n * CUT, (n + 1) * CUT)
         made = dot(own_block, qkv_w[0, :, cols]).astype(BF16)
         query[:, cols] = made * jnp.asarray(1.0 / math.sqrt(HEAD), BF16)
-    keys_values(own_low, FRAMES)
-    for distance in (1, 2):
-        for k in range(2):
-            for d in (-distance, distance):
-                near_copy(d, k).wait_recv()
-                if distance == 1:
-                    near_copy(2 * d, k).start()
-                share_copy(d, k).start()
-        for d in (-distance, distance):
-            for k in range(2):
-                share_copy(d, k).wait_recv()
-            keys_values((REACH + d) * FRAMES, FRAMES)
-
+    keys_values([own_low])
     lane_low = lax.broadcasted_iota(jnp.int32, (FRAMES, 128), 1) < HEAD
 
-    def attend(pair, carry):
+    def pair_scores(pair, pieces_of):
         cols = pl.ds(pl.multiple_of(pair * 128, 128), 128)
         both = query[:, cols]
         zero = jnp.zeros_like(both)
         stacked = jnp.concatenate(
             [jnp.where(lane_low, both, zero), jnp.where(lane_low, zero, both)], axis=0
         )
+        near_keys = jnp.concatenate([keys[rows, cols] for rows in pieces_of], axis=0)
+        near_values = jnp.concatenate([values[rows, cols] for rows in pieces_of], axis=0)
+        mask = jnp.concatenate([bias_mask[:, rows] for rows in pieces_of], axis=1)
         scores = lax.dot_general(
-            stacked, keys[:, cols], (((1,), (1,)), ((), ())), preferred_element_type=F32
-        )
-        mask = bias_mask[...]
-        scores = scores + jnp.concatenate([mask, mask], axis=0)
+            stacked, near_keys, (((1,), (1,)), ((), ())), preferred_element_type=F32
+        )
+        return scores + jnp.concatenate([mask, mask], axis=0), near_values
+
+    middle = [slice(FRAMES, 4 * FRAMES)]
+    far = [slice(0, FRAMES), slice(4 * FRAMES, 5 * FRAMES)]
+
+    def attend_middle(pair, carry):
+        scores, near_values = pair_scores(pair, middle)
         highest = jnp.max(scores, axis=1, keepdims=True)
         weight = jnp.exp(scores - highest)
+        highest_mid[pair] = jnp.broadcast_to(highest, (2 * FRAMES, 128))
         denominator = jnp.sum(weight, axis=1, keepdims=True)
-        mixed = dot(weight.astype(BF16), values[:, cols]) / denominator
+        denominator_mid[pair] = jnp.broadcast_to(denominator, (2 * FRAMES, 128))
+        numerator_mid[pair] = dot(weight.astype(BF16), near_values)
+        return carry
+
+    def attend_far(pair, carry):
+        scores, near_values = pair_scores(pair, far)
+        before = highest_mid[pair]
+        highest = jnp.maximum(before, jnp.max(scores, axis=1, keepdims=True))
+        factor = jnp.exp(before - highest)
+        weight = jnp.exp(scores - jnp.concatenate([highest, highest], axis=1))
+        denominator = denominator_mid[pair] * factor + jnp.sum(weight, axis=1, keepdims=True)
+        numerator = numerator_mid[pair] * factor + dot(weight.astype(BF16), near_values)
+        mixed = numerator / denominator
+        cols = pl.ds(pl.multiple_of(pair * 128, 128), 128)
         context[:, cols] = jnp.where(lane_low, mixed[:FRAMES], mixed[FRAMES:]).astype(BF16)
         return carry
 
-    lax.fori_loop(0, LOCAL // 128, attend, 0)
+    for k in range(2):
+        for d in (-1, 1):
+            near_copy(d, k).wait_recv()
+            near_copy(2 * d, k).start()
+            share_copy(d, k).start()
+    for k in range(2):
+        for d in (-1, 1):
+            share_copy(d, k).wait_recv()
+    keys_values([FRAMES, 3 * FRAMES])
+    lax.fori_loop(0, LOCAL // 128, attend_middle, 0)
+    for k in range(2):
+        for d in (-2, 2):
+            near_copy(d, k).wait_recv()
+            share_copy(d, k).start()
+    for k in range(2):
+        for d in (-2, 2):
+            share_copy(d, k).wait_recv()
+    keys_values([0, 4 * FRAMES])
+    lax.fori_loop(0, LOCAL // 128, attend_far, 0)
 
     def br_copy(n):
         return remote(br_out.at[n], br_in.at[n], br_send.at[n], br_recv.at[n], {"phase": other})
@@ -628,6 +681,8 @@
         pltpu.VMEM((768, 128), BF16),
         pltpu.VMEM((4, ROWS, 256), BF16),
         pltpu.VMEM((5, ROWS, 256), BF16),
+        pltpu.VMEM((4, ROWS, 256), BF16),
+        pltpu.VMEM((5, ROWS, 256), BF16),
         pltpu.VMEM((TILES, 128, WIDTH), BF16),
         pltpu.VMEM((SIDE, TILES, FRAMES, 128), BF16),
         pltpu.VMEM((SIDE, TILES, FRAMES, 128), BF16),
@@ -646,6 +701,9 @@
         pltpu.VMEM((SPAN, LOCAL), BF16),
         pltpu.VMEM((SPAN, LOCAL), BF16),
         pltpu.VMEM((FRAMES, SPAN), F32),
+        pltpu.VMEM((6, 2 * FRAMES, 128), F32),
+        pltpu.VMEM((6, 2 * FRAMES, 128), F32),
+        pltpu.VMEM((6, 2 * FRAMES, 128), F32),
         pltpu.VMEM((FRAMES, LOCAL), BF16),
         pltpu.VMEM((3, FRAMES, CUT), BF16),
         pltpu.VMEM((3, FRAMES, CUT), BF16),

time: 68.6 us -> 71.3 us (1.039)
  Pallas kernels: 66.9 us -> 69.6 us
    pallas_call x1, Pallas kernels: 66.9 us -> 69.6 us  [local(): pl.pallas_call(body, out_shape=jax.ShapeDtypeStruct((FRAMES, LOCAL), BF16...]
where the time goes in v3:
time: 71.3 us; the launch traced here: 71.2 us
  Pallas kernels  69.6 us (98%)
  local copies, waits for them, and re-layouts  1.62 us (2%)
    pallas_call x1, Pallas kernels, local(): pl.pallas_call(body, out_shape=jax.ShapeDtypeStruct((FRAMES, LOCAL), BF16...  69.6 us
    unnamed x1, local copies, waits for them, and re-layouts  1.62 us

profile of v3, /device:TPU:1, one launch (start us, length us, event | category | flops | bytes accessed | tf_op | source)
XLA Modules:
  0.0 71.2 jit_solution(577858444418415710)
XLA Ops:
  0.0 69.6 %shard_map.109 = bf16[128,768]{1,0:T(8,128)(2,1)} custom-call(s32[1,12]{1,0:T(1,128)} %lengths_ref.1, bf16[512,128]{1,0:T(8,128)(2,1)} %bitcast.9, f32[3,3,256]{2,1,0:T(4,128)} %w1_hbm.1, f32[2,128]{1,0:T(2,128)} %bitcast.12, bf16[3,3,256,128]{3,2,1,0:T(8,128)(2,1)} %w2_ref.1, f32[1,128]{1,0:T(1,128)} %bitcast.13, bf16[256,1536]{1,0:T(8,128)(2,1)} %wp_hbm.1, ...), custom_call_target="tpu_custom_call" | custom-call | tf_op jit(solution)/shard_map/pallas_call | solution.py:735
  69.6 1.6 %copy.13 = bf16[1,128,768]{2,1,0:T(8,128)(2,1)} copy(bf16[1,128,768]{2,1,0:T(8,128)(2,1)} %bitcast.8) | data formatting | bytes 393216

commit v4 on v2

--- a/solution.py
+++ b/solution.py
@@ -117,7 +117,7 @@
     x = block % SIDE
     y = block // SIDE
     plane = lax.axis_index("batch")
-    planes = lax.axis_size("batch")
+    partner = plane + 1 - 2 * (plane % 2)
     other = 1 - phase
 
     def row_of(ref):
@@ -128,9 +128,6 @@
 
     def column_peer(dy):
         return ((y + dy + SIDE) % SIDE) * SIDE + x
-
-    def plane_peer(dz):
-        return (plane + dz + planes) % planes
 
     def near_peer(d):
         return (block + d + BLOCKS) % BLOCKS
@@ -184,7 +181,7 @@
     peers = [{"phase": other}]
     peers += [{"seq": row_peer(dx)} for dx in range(1, SIDE)]
     peers += [{"seq": column_peer(dy)} for dy in (1, 3)]
-    peers += [{"batch": plane_peer(dz)} for dz in (1, -1)]
+    peers += [{"batch": partner}]
     peers += [{"seq": near_peer(d)} for d in (1, -1)]
     for peer in peers:
         pl.semaphore_signal(barrier, inc=1, device_id=peer, device_id_type=MESH)
@@ -208,36 +205,43 @@
     )
     halo_copy.start()
     drain = [halo_copy.wait_send]
-    half_low = (plane % 2) * 4
-    pieces = [
-        (-1, 0, 1),
-        (1, 1, -1),
-        (-1, 1, -1),
-        (1, 0, 1),
-        (2, 0, 1),
-        (2, 1, -1),
+    own_groups = 2 * (plane % 2)
+    along_y = [
+        (-1, own_groups, 2, -1),
+        (1, own_groups, 2, 1),
+        (-1, 4, 2, -1),
+        (1, 6, 2, 1),
+        (-1, 6, 2, -1),
+        (1, 4, 2, 1),
+        (2, own_groups, 1, -1),
+        (2, own_groups + 1, 1, 1),
+        (2, 4, 2, -1),
+        (2, 6, 2, 1),
     ]
-
-    def w_piece(dy, part_of, low):
+    along_z = [
+        (-1, own_groups, 2),
+        (1, own_groups, 2),
+        (2, own_groups, 1),
+        (2, own_groups + 1, 1),
+    ]
+
+    def w_piece(dy, low, groups):
         rows = pl.ds(pl.multiple_of(((y + dy + SIDE) % SIDE) * 32, 32), 32)
-        return w_all.at[pl.ds(low + 2 * part_of, 2), rows, :]
+        return w_all.at[pl.ds(low, groups), rows, :]
 
     def w_along_y(k):
-        dy, part_of, _ = pieces[k]
-        step = -1 if dy == -1 or (dy == 2 and part_of == 0) else 1
-        mine = w_piece(dy - step, part_of, half_low)
-        return remote(
-            mine, mine, wy_send.at[k], wy_recv.at[k], {"seq": column_peer(-step)}
-        )
+        dy, low, groups, side = along_y[k]
+        piece = w_piece(dy - side, low, groups)
+        return remote(piece, piece, wy_send.at[k], wy_recv.at[k], {"seq": column_peer(-side)})
 
     def w_along_z(k):
-        dy, part_of, dz = pieces[k]
-        mine = w_piece(dy, part_of, half_low)
-        return remote(mine, mine, wz_send.at[k], wz_recv.at[k], {"batch": plane_peer(dz)})
+        piece = w_piece(*along_z[k])
+        return remote(piece, piece, wz_send.at[k], wz_recv.at[k], {"batch": partner})
 
     def w_sent():
-        for k in range(6):
+        for k in range(10):
             w_along_y(k).wait_send()
+        for k in range(4):
             w_along_z(k).wait_send()
 
     drain.append(w_sent)
@@ -245,11 +249,21 @@
         w_along_y(k).start()
 
     def w_step(step):
-        for k in (2 * step, 2 * step + 1):
-            w_along_y(k).wait_recv()
-            if step == 0:
-                w_along_y(4 + k).start()
-            w_along_z(k).start()
+        if step == 0:
+            for k in (0, 1):
+                w_along_y(k).wait_recv()
+                w_along_y(6 + k).start()
+                w_along_z(k).start()
+            for k in (4, 5):
+                w_along_y(k).start()
+        if step == 1:
+            for k in (2, 3):
+                w_along_y(k).wait_recv()
+                w_along_y(6 + k).start()
+        if step == 2:
+            for k in (6, 7):
+                w_along_y(k).wait_recv()
+                w_along_z(k - 4).start()
 
     offsets = []
     running = jnp.int32(0)
@@ -399,8 +413,10 @@
         return carry
 
     lax.fori_loop(0, TILES, maps_wait, 0)
-    for k in range(6):
+    for k in range(4):
         w_along_z(k).wait_recv()
+    for k in (4, 5, 8, 9):
+        w_along_y(k).wait_recv()
 
     mine = pl.ds(pl.multiple_of(phase * HALF, HALF), HALF)
     theirs = pl.ds(pl.multiple_of(other * HALF, HALF), HALF)
@@ -655,10 +671,10 @@
         dma,
         dma,
         dma,
-        dma((6,)),
-        dma((6,)),
-        dma((6,)),
-        dma((6,)),
+        dma((10,)),
+        dma((10,)),
+        dma((4,)),
+        dma((4,)),
         dma((3, TILES)),
         dma((3, TILES)),
         dma((CUTS,)),

time: 68.6 us -> 64.3 us (0.937)
  Pallas kernels: 66.9 us -> 62.6 us
    pallas_call x1, Pallas kernels: 66.9 us -> 62.6 us  [local(): pl.pallas_call(body, out_shape=jax.ShapeDtypeStruct((FRAMES, LOCAL), BF16...]
where the time goes in v4:
time: 64.3 us; the launch traced here: 64.2 us
  Pallas kernels  62.6 us (97%)
  local copies, waits for them, and re-layouts  1.62 us (3%)
    pallas_call x1, Pallas kernels, local(): pl.pallas_call(body, out_shape=jax.ShapeDtypeStruct((FRAMES, LOCAL), BF16...  62.6 us
    unnamed x1, local copies, waits for them, and re-layouts  1.62 us

profile of v4, /device:TPU:1, one launch (start us, length us, event | category | flops | bytes accessed | tf_op | source)
XLA Modules:
  0.0 64.2 jit_solution(8676248178385225543)
XLA Ops:
  0.0 62.6 %shard_map.109 = bf16[128,768]{1,0:T(8,128)(2,1)} custom-call(s32[1,12]{1,0:T(1,128)} %lengths_ref.1, bf16[512,128]{1,0:T(8,128)(2,1)} %bitcast.9, f32[3,3,256]{2,1,0:T(4,128)} %w1_hbm.1, f32[2,128]{1,0:T(2,128)} %bitcast.12, bf16[3,3,256,128]{3,2,1,0:T(8,128)(2,1)} %w2_ref.1, f32[1,128]{1,0:T(1,128)} %bitcast.13, bf16[256,1536]{1,0:T(8,128)(2,1)} %wp_hbm.1, ...), custom_call_target="tpu_custom_call" | custom-call | tf_op jit(solution)/shard_map/pallas_call | solution.py:693
  62.6 1.6 %copy.13 = bf16[1,128,768]{2,1,0:T(8,128)(2,1)} copy(bf16[1,128,768]{2,1,0:T(8,128)(2,1)} %bitcast.8) | data formatting | bytes 393216

commit v5 on v4

--- a/solution.py
+++ b/solution.py
@@ -75,6 +75,8 @@
     tot,
     rs_out,
     rs_in,
+    relay_in,
+    relay_out,
     frames_mine,
     frames_cols,
     normed,
@@ -124,7 +126,7 @@
         return jnp.concatenate([ref[k : k + 1, :] for k in range(WIDTH // 128)], axis=1)
 
     def row_peer(dx):
-        return y * SIDE + (x + dx) % SIDE
+        return y * SIDE + (x + dx + SIDE) % SIDE
 
     def column_peer(dy):
         return ((y + dy + SIDE) % SIDE) * SIDE + x
@@ -426,14 +428,41 @@
             sib_out.at[n], sib_in.at[n], sib_send.at[n], sib_recv.at[n], {"phase": other}
         )
 
-    def rs_copy(dx, n):
+    def way(n):
+        return 1 - 2 * (n % 2)
+
+    def through_copy(n):
         return remote(
-            rs_out.at[n, (x + dx) % SIDE],
-            rs_in.at[dx - 1, n],
-            rs_send.at[dx - 1, n],
-            rs_recv.at[dx - 1, n],
-            {"seq": row_peer(dx)},
-        )
+            rs_out.at[n, (x + 2) % SIDE],
+            relay_in.at[n],
+            rs_send.at[2, n],
+            rs_recv.at[2, n],
+            {"seq": row_peer(way(n))},
+        )
+
+    def back_copy(n):
+        return remote(
+            rs_out.at[n, (x - way(n) + SIDE) % SIDE],
+            rs_in.at[0, n],
+            rs_send.at[0, n],
+            rs_recv.at[0, n],
+            {"seq": row_peer(-way(n))},
+        )
+
+    def joint_copy(n):
+        return remote(
+            relay_out.at[n],
+            rs_in.at[1, n],
+            rs_send.at[1, n],
+            rs_recv.at[1, n],
+            {"seq": row_peer(way(n))},
+        )
+
+    def relay(n):
+        through_copy(n).wait_recv()
+        added = tot[n, (x + way(n) + SIDE) % SIDE] + relay_in[n].astype(F32)
+        relay_out[n] = added.astype(BF16)
+        joint_copy(n).start()
 
     def project(n):
         cols = pl.ds(pl.multiple_of(n * CUT, CUT), CUT)
@@ -454,40 +483,42 @@
         both = part[n, :, mine, :] + sib_in[n].astype(F32)
         tot[n] = both
         rs_out[n] = both.astype(BF16)
-        for dx in (2, 1, 3):
-            rs_copy(dx, n).start()
+        through_copy(n).start()
+        back_copy(n).start()
 
     def project_step(n, carry):
         @pl.when(n < CUTS)
         def _():
             project(n)
 
-        @pl.when(n >= 2)
+        @pl.when((n >= 2) & (n < CUTS + 2))
         def _():
             pass_on(n - 2)
+
+        @pl.when(n >= 5)
+        def _():
+            relay(n - 5)
 
         return carry
 
     def sums_sent():
         def step(n, carry):
             sib_copy(n).wait_send()
-            for dx in range(1, SIDE):
-                rs_copy(dx, n).wait_send()
+            for copy in (through_copy, back_copy, joint_copy):
+                copy(n).wait_send()
             return carry
 
         lax.fori_loop(0, CUTS, step, 0)
 
     drain.append(sums_sent)
-    lax.fori_loop(0, CUTS + 2, project_step, 0)
+    lax.fori_loop(0, CUTS + 5, project_step, 0)
 
     proj_bias = row_of(pb_ref)
     for n in range(CUTS):
         cols = slice(n * CUT, (n + 1) * CUT)
-        for dx in range(1, SIDE):
-            rs_copy(dx, n).wait_recv()
-        total = tot[n, x]
-        for dx in range(1, SIDE):
-            total = total + rs_in[dx - 1, n].astype(F32)
+        back_copy(n).wait_recv()
+        joint_copy(n).wait_recv()
+        total = tot[n, x] + rs_in[0, n].astype(F32) + rs_in[1, n].astype(F32)
         frames_mine[:, cols] = (total + proj_bias[:, cols]).astype(BF16)
     frames_copy = remote(
         frames_mine.at[:, pl.ds(pl.multiple_of(other * LOCAL, LOCAL), LOCAL)],
@@ -652,7 +683,9 @@
         pltpu.VMEM((CUTS, SIDE, HALF, CUT), BF16),
         pltpu.VMEM((CUTS, SIDE, HALF, CUT), F32),
         pltpu.VMEM((CUTS, SIDE, HALF, CUT), BF16),
-        pltpu.VMEM((SIDE - 1, CUTS, HALF, CUT), BF16),
+        pltpu.VMEM((2, CUTS, HALF, CUT), BF16),
+        pltpu.VMEM((CUTS, HALF, CUT), BF16),
+        pltpu.VMEM((CUTS, HALF, CUT), BF16),
         pltpu.VMEM((HALF, WIDTH), BF16),
         pltpu.VMEM((FRAMES, LOCAL), BF16),
         pltpu.VMEM((SPAN, WIDTH), BF16),

time: 64.3 us -> 63.1 us (0.981)
  Pallas kernels: 62.6 us -> 61.4 us
    pallas_call x1, Pallas kernels: 62.6 us -> 61.4 us  [local(): pl.pallas_call(body, out_shape=jax.ShapeDtypeStruct((FRAMES, LOCAL), BF16...]
where the time goes in v5:
time: 63.1 us; the launch traced here: 63 us
  Pallas kernels  61.4 us (97%)
  local copies, waits for them, and re-layouts  1.62 us (3%)
    pallas_call x1, Pallas kernels, local(): pl.pallas_call(body, out_shape=jax.ShapeDtypeStruct((FRAMES, LOCAL), BF16...  61.4 us
    unnamed x1, local copies, waits for them, and re-layouts  1.62 us

profile of v5, /device:TPU:1, one launch (start us, length us, event | category | flops | bytes accessed | tf_op | source)
XLA Modules:
  0.0 63.0 jit_solution(377221912562523154)
XLA Ops:
  0.0 61.4 %shard_map.109 = bf16[128,768]{1,0:T(8,128)(2,1)} custom-call(s32[1,12]{1,0:T(1,128)} %lengths_ref.1, bf16[512,128]{1,0:T(8,128)(2,1)} %bitcast.9, f32[3,3,256]{2,1,0:T(4,128)} %w1_hbm.1, f32[2,128]{1,0:T(2,128)} %bitcast.12, bf16[3,3,256,128]{3,2,1,0:T(8,128)(2,1)} %w2_ref.1, f32[1,128]{1,0:T(1,128)} %bitcast.13, bf16[256,1536]{1,0:T(8,128)(2,1)} %wp_hbm.1, ...), custom_call_target="tpu_custom_call" | custom-call | tf_op jit(solution)/shard_map/pallas_call | solution.py:726
  61.4 1.6 %copy.13 = bf16[1,128,768]{2,1,0:T(8,128)(2,1)} copy(bf16[1,128,768]{2,1,0:T(8,128)(2,1)} %bitcast.8) | data formatting | bytes 393216
